TPU v7x, 512 devices: a whole 4x8x8 slice. The times are simulated.
512 devices in a mesh: row: 8 (over y), col: 8 (over z), depth: 8 (over x, core).
Axes of the slice: x: 4, y: 8, z: 8, core: 2. Of those that a mesh axis runs over, the one named last changes fastest.
Arguments:
- tokens: bfloat16 [256, 12288], P(('col', 'depth'), 'row'), may hold values from -6 to 6
- weight_in: bfloat16 [12288, 24576], P('row', ('col', 'depth')), may hold values from -0.0546875 to 0.0546875
- weight_out: bfloat16 [24576, 12288], P(('col', 'depth'), 'row'), may hold values from -0.0390625 to 0.0390625
- cotangent: bfloat16 [256, 12288], P(('col', 'depth'), 'row'), may hold values from -6 to 6
Outputs:
- output: bfloat16 [256, 12288], P(('col', 'depth'), 'row')
- grad_tokens: bfloat16 [256, 12288], P(('col', 'depth'), 'row')
- grad_weight_in: bfloat16 [12288, 24576], P('row', ('col', 'depth'))
- grad_weight_out: bfloat16 [24576, 12288], P(('col', 'depth'), 'row')
All inputs are finite; a program needn't handle non-finite values.
Results may differ from a plain program's by a relative error of at most 0.0049.
Values may be sent and summed in bfloat16 or wider, within the bound.
No kernel may reach another device: no remote copies, remote signals or barrier semaphores. Data moves between devices by JAX's collectives and lax.ppermute only.
A program may use at most 64 MiB of HBM per device.

v0:
```python
import math

import jax
import jax.numpy as jnp
from jax import lax
from jax.sharding import PartitionSpec as P

root_two_pi = math.sqrt(2.0 / math.pi)
cubic = 0.044715


def gelu_value(hidden):
    inner = jnp.tanh(root_two_pi * (hidden + cubic * hidden * hidden * hidden))
    return 0.5 * hidden * (1.0 + inner)


def gelu_slope(hidden):
    inner = jnp.tanh(root_two_pi * (hidden + cubic * hidden * hidden * hidden))
    return 0.5 * (1.0 + inner) + 0.5 * hidden * (1.0 - inner * inner) * root_two_pi * (
        1.0 + 3.0 * cubic * hidden * hidden
    )


def inner_last(left, right):
    return lax.dot_general(
        left, right, (((1,), (1,)), ((), ())), preferred_element_type=jnp.float32
    )


def inner_first(left, right):
    return lax.dot_general(
        left, right, (((0,), (0,)), ((), ())), preferred_element_type=jnp.float32
    )


def local(tokens, weight_in, weight_out, cotangent):
    gathered = lax.all_gather(tokens, ("col", "depth"), axis=0, tiled=True)
    partial_value = jnp.dot(gathered, weight_in, preferred_element_type=jnp.float32)
    hidden = lax.psum(partial_value, "row")
    active = gelu_value(hidden).astype(jnp.bfloat16)
    out_terms = jnp.dot(active, weight_out, preferred_element_type=jnp.float32)
    output = lax.psum_scatter(out_terms, ("col", "depth"), scatter_dimension=0, tiled=True)
    output = output.astype(jnp.bfloat16)
    grad_rows = lax.all_gather(cotangent, ("col", "depth"), axis=0, tiled=True)
    slope_terms = inner_last(grad_rows, weight_out)
    grad_active = lax.psum(slope_terms, "row")
    grad_hidden = (grad_active * gelu_slope(hidden)).astype(jnp.bfloat16)
    grad_weight_out = inner_first(active, grad_rows).astype(jnp.bfloat16)
    back_terms = inner_last(grad_hidden, weight_in)
    grad_tokens = lax.psum_scatter(back_terms, ("col", "depth"), scatter_dimension=0, tiled=True)
    grad_tokens = grad_tokens.astype(jnp.bfloat16)
    grad_weight_in = inner_first(gathered, grad_hidden).astype(jnp.bfloat16)
    return (output, grad_tokens, grad_weight_in, grad_weight_out)


def solution(mesh):
    placed = (
        P(("col", "depth"), "row"),
        P("row", ("col", "depth")),
        P(("col", "depth"), "row"),
        P(("col", "depth"), "row"),
    )
    return jax.shard_map(
        local,
        mesh=mesh,
        in_specs=placed,
        out_specs=(
            P(("col", "depth"), "row"),
            P(("col", "depth"), "row"),
            P("row", ("col", "depth")),
            P(("col", "depth"), "row"),
        ),
        check_vma=False,
    )
```

profile of v0, /device:TPU:8, one launch (start us, length us, event | category | flops | bytes accessed | tf_op | source)
XLA Modules:
  0.0 491.7 jit_solution(10291953272173501184)
XLA Ops:
  7.2 0.0 copy-start
  7.2 0.0 all-reduce.7.cloned.1.call-start
  7.2 0.0 copy-start.6
  7.2 56.8 %all-gather.1 = bf16[64,4,1536]{2,1,0:T(4,128)(2,1)S(1)} all-gather(bf16[1,4,1536]{2,1,0:T(4,128)(2,1)} %bitcast.15), channel_id=1, replica_groups=mesh['row'=8,'col'=8,'depth'=8] {'col','depth'}, dimensions={0}, use_global_device_ids=true | all-gather | bytes 798720 | tf_op jit(solution)/shard_map/all_gather | solution.py:44
  64.0 0.2 reshape.11
  64.2 0.0 copy-done.6
  64.2 49.7 %all-gather = bf16[64,4,1536]{2,1,0:T(4,128)(2,1)S(1)} all-gather(bf16[1,4,1536]{2,1,0:T(4,128)(2,1)S(1)} %bitcast.16), channel_id=1, replica_groups=mesh['row'=8,'col'=8,'depth'=8] {'col','depth'}, dimensions={0}, use_global_device_ids=true | all-gather | bytes 798720 | tf_op jit(solution)/shard_map/all_gather | solution.py:37
  113.9 0.2 reshape.9
  114.1 0.0 copy-done
  114.1 0.0 copy-start.2
  114.1 1.3 fusion.10
  115.4 0.0 copy-done.2
  115.4 1.3 fusion.9
  116.8 0.0 all-reduce.7.cloned.1.call-update
  116.8 1.3 dynamic-slice
  118.7 73.9 %all-reduce.7.cloned.1.call-done = (f32[256,384]{1,0:T(8,128)}, f32[256,384]{1,0:T(8,128)}) async-done(((f32[256,384]{1,0:T(8,128)}, f32[256,384]{1,0:T(8,128)}), (f32[256,384]{1,0:T(8,128)}, f32[256,384]{1,0:T(8,128)})) %all-reduce.7.cloned.1.call-update) | async-done | bytes 786448 | tf_op jit(solution)/shard_map/psum | solution.py:39
  192.6 0.0 copy-start.4
  192.6 0.0 copy-start.5
  192.6 0.0 copy-start.3
  192.6 2.9 fusion.8
  195.4 0.0 copy-done.4
  195.4 0.0 copy-done.5
  195.4 0.3 fusion.7
  195.7 0.0 copy-done.3
  195.7 1.8 fusion.11
  197.5 1.5 fusion
  199.0 1.6 convolution_convert_fusion
  200.6 0.0 copy-start.1
  200.6 2.5 copy.9
  203.1 0.0 copy-done.1
  203.1 280.5 %all-reduce.8 = (bf16[256,1536]{1,0:T(8,128)(2,1)S(1)}, bf16[256,1536]{1,0:T(8,128)(2,1)}) all-reduce(f32[256,1536]{1,0:T(8,128)S(1)} %copy-done.1, f32[256,1536]{1,0:T(8,128)} %fusion.11), channel_id=2, replica_groups=mesh['row'=8,'col'=8,'depth'=8] {'col','depth'}, use_global_device_ids=true, to_apply=%region_1.0.clone | all-reduce | flops 786432 | bytes 4718592
  483.5 1.4 dynamic-slice_convert_fusion
Async XLA Ops:
  7.2 106.9 %copy-start = (bf16[384,1536]{1,0:T(8,128)(2,1)S(1)}, bf16[384,1536]{1,0:T(8,128)(2,1)}, u32[]{:S(2)}) copy-start(bf16[384,1536]{1,0:T(8,128)(2,1)} %param.6) | copy-start | bytes 3538948
  7.2 185.4 %all-reduce.7.cloned.1.call-start = ((), (), s32[]{:S(2)}) async-start(), calls=%async_computation | async-start | bytes 1572864 | tf_op jit(solution)/shard_map/psum | solution.py:39
  7.2 57.0 %copy-start.6 = (bf16[4,1536]{1,0:T(4,128)(2,1)S(1)}, bf16[4,1536]{1,0:T(4,128)(2,1)}, u32[]{:S(2)}) copy-start(bf16[4,1536]{1,0:T(4,128)(2,1)} %param.4) | copy-start | bytes 36868
  114.1 1.4 copy-start.2
  192.6 2.9 copy-start.4
  192.6 2.9 copy-start.5
  192.6 3.1 copy-start.3
  200.6 2.5 copy-start.1
Sparse Core Ops, SparseCore 0:
  116.9 75.6 all-reduce.6
where the time goes:
time: 492 us
  blocking collectives  387 us (79%)
  waiting for transfers between devices  73.9 us (15%)
  between operations  14.8 us (3%)
  matrix products  10.4 us (2%)
  local copies, waits for them, and re-layouts  5.5 us (1%)
    unnamed x1, blocking collectives  280 us
    psum x1, waiting for transfers between devices, local(): hidden = lax.psum(partial_value, 'row')  73.9 us
    all_gather x1, blocking collectives, local(): grad_rows = lax.all_gather(cotangent, ('col', 'depth'), axis=0, tiled=True)  56.8 us
    all_gather x1, blocking collectives, local(): gathered = lax.all_gather(tokens, ('col', 'depth'), axis=0, tiled=True)  49.7 us
  transfers between devices with their start and end apart: 1, of which 1 were waited for; matrix products, arithmetic and copies ran while one was open for 0% of the time, Pallas kernels for 0%

commit v1 on v0

v1 whole, which is shorter than its diff:
```python
import math

import jax
import jax.numpy as jnp
from jax import lax
from jax.sharding import Mesh, PartitionSpec as P

root_two_pi = math.sqrt(2.0 / math.pi)
cubic = 0.044715
chips = ("col", "x")


def gelu_parts(hidden):
    inner = jnp.tanh(root_two_pi * (hidden + cubic * hidden * hidden * hidden))
    value = 0.5 * hidden * (1.0 + inner)
    slope = 0.5 * (1.0 + inner) + 0.5 * hidden * (1.0 - inner * inner) * root_two_pi * (
        1.0 + 3.0 * cubic * hidden * hidden
    )
    return value, slope


def inner_last(left, right):
    return lax.dot_general(
        left, right, (((1,), (1,)), ((), ())), preferred_element_type=jnp.float32
    )


def inner_first(left, right):
    return lax.dot_general(
        left, right, (((0,), (0,)), ((), ())), preferred_element_type=jnp.float32
    )


def plain(left, right):
    return jnp.dot(left, right, preferred_element_type=jnp.float32)


def other_core(block):
    return lax.ppermute(block, "core", [(0, 1), (1, 0)])


def exchange(blocks, axes):
    return lax.all_to_all(blocks, axes, split_axis=0, concat_axis=0)


def copies(block, count):
    return jnp.broadcast_to(block[None], (count,) + block.shape)


def local(tokens, weight_in, weight_out, cotangent):
    bf16 = jnp.bfloat16
    rows = lax.axis_size("row")
    count = lax.axis_size("col") * lax.axis_size("x")
    share, width = tokens.shape
    units = weight_in.shape[1]
    half = count * share

    both = jnp.concatenate([tokens, cotangent], axis=0)
    mine = exchange(copies(both, count), chips)
    theirs = other_core(mine)

    def split(block):
        return block[:, :share].reshape(half, width), block[:, share:].reshape(half, width)

    tokens_mine, grad_mine = split(mine)
    tokens_theirs, grad_theirs = split(theirs)

    def terms(tok, grad):
        return jnp.concatenate(
            [plain(tok, weight_in).astype(bf16), inner_last(grad, weight_out).astype(bf16)], axis=1
        )

    partial = jnp.concatenate(
        [terms(tokens_mine, grad_mine), terms(tokens_theirs, grad_theirs)], axis=0
    )
    received = exchange(partial.reshape(rows, 2 * half // rows, 2 * units), "row")
    total = jnp.sum(received.astype(jnp.float32), axis=0)
    value, slope = gelu_parts(total[:, :units])
    acts = jnp.concatenate(
        [value.astype(bf16), (total[:, units:] * slope).astype(bf16)], axis=1
    )
    acts = exchange(copies(acts, rows), "row").reshape(2 * half, 2 * units)
    active, grad_hidden = acts[:, :units], acts[:, units:]

    def products(rows_of):
        return jnp.stack(
            [
                plain(active[rows_of], weight_out).reshape(count, share, width),
                inner_last(grad_hidden[rows_of], weight_in).reshape(count, share, width),
            ],
            axis=1,
        ).reshape(count, 2 * share, width)

    sent = other_core(products(slice(half, 2 * half)).astype(bf16))
    kept = products(slice(0, half))
    summed = (kept + sent.astype(jnp.float32)).astype(bf16)
    blocks = exchange(summed, chips)
    final = jnp.sum(blocks.astype(jnp.float32), axis=0).astype(bf16)

    tokens_all = jnp.concatenate([tokens_mine, tokens_theirs], axis=0)
    grad_all = jnp.concatenate([grad_mine, grad_theirs], axis=0)
    grad_weight_in = inner_first(tokens_all, grad_hidden).astype(bf16)
    grad_weight_out = inner_first(active, grad_all).astype(bf16)
    return final[:share], final[share:], grad_weight_in, grad_weight_out


def solution(mesh):
    sizes = dict(mesh.shape)
    finer = Mesh(
        mesh.devices.reshape(sizes["row"], sizes["col"], sizes["depth"] // 2, 2),
        ("row", "col", "x", "core"),
    )
    wide = ("col", "x", "core")
    placed = (P(wide, "row"), P("row", wide), P(wide, "row"), P(wide, "row"))
    return jax.shard_map(
        local,
        mesh=finer,
        in_specs=placed,
        out_specs=(P(wide, "row"), P(wide, "row"), P("row", wide), P(wide, "row")),
        check_vma=False,
    )
```

time: 492 us -> 134 us (0.27)
  the two profiles are of different devices: /device:TPU:8 before, /device:TPU:2 now
where the time goes in v1:
time: 134 us
  blocking collectives  75.5 us (56%)
  waiting for transfers between devices  19.9 us (15%)
  local copies, waits for them, and re-layouts  14.1 us (11%)
  matrix products  10.2 us (8%)
  starting transfers between devices  9.52 us (7%)
  other arithmetic  3.56 us (3%)
    all_to_all x3, blocking collectives, exchange(): return lax.all_to_all(blocks, axes, split_axis=0, concat_axis=0)  75.5 us
    all_to_all x1, waiting for transfers between devices, exchange(): return lax.all_to_all(blocks, axes, split_axis=0, concat_axis=0)  19.9 us
    all_to_all x1, starting transfers between devices, exchange(): return lax.all_to_all(blocks, axes, split_axis=0, concat_axis=0)  5.7 us
    another operation x8, local copies, waits for them, and re-layouts, products(): jnp.stack([plain(active[rows_of], weight_out).reshape(count, share, width...  4.28 us
    dot_general x4, matrix products, inner_last(): lax.dot_general(left, right, (((1,), (1,)), ((), ())), preferred_element_...  4.18 us
    ppermute x2, starting transfers between devices, other_core(): return lax.ppermute(block, 'core', [(0, 1), (1, 0)])  3.82 us
    dot_general x2, matrix products, inner_first(): lax.dot_general(left, right, (((0,), (0,)), ((), ())), preferred_element_...  3.12 us
    dot_general x4, matrix products, plain(): return jnp.dot(left, right, preferred_element_type=jnp.float32)  2.86 us
  transfers between devices with their start and end apart: 3, of which 1 were waited for; matrix products, arithmetic and copies ran while one was open for 11% of the time, Pallas kernels for 0%

profile of v1, /device:TPU:2, one launch (start us, length us, event | category | flops | bytes accessed | tf_op | source)
XLA Modules:
  0.0 133.7 jit_solution(7266470530646516093)
XLA Ops:
  0.6 0.0 copy-start
  0.6 0.8 pad_maximum_fusion.3
  1.5 0.1 broadcast_in_dim.4
  1.5 35.7 %all_to_all.20 = bf16[32,8,1536]{2,1,0:T(8,128)(2,1)S(1)} all-to-all(bf16[32,8,1536]{2,1,0:T(8,128)(2,1)S(1)} %broadcast_in_dim.4), channel_id=1, replica_groups=mesh['row'=8,'col'=8,'x'=4,'core'=2] {'col','x'}, dimensions={0} | all-to-all | bytes 1572864 | tf_op jit(solution)/shard_map/all_to_all | solution.py:43
  37.3 1.9 %collective-permute-start = (bf16[32,8,1536]{2,1,0:T(8,128)(2,1)S(1)}, bf16[32,8,1536]{2,1,0:T(8,128)(2,1)}, u32[]{:S(2)}, u32[]{:S(2)}) collective-permute-start(bf16[32,8,1536]{2,1,0:T(8,128)(2,1)S(1)} %all_to_all.20), channel_id=1, source_target_pairs={{0,1},{1,0},{2,3},{3,2},{4,5},{5,4},{6,7},{7,6},{8,9},{9,8},{10,11... | collective-permute-start | bytes 2359304 | tf_op jit(solution)/shard_map/ppermute | solution.py:39
  39.2 1.1 fusion.24
  40.3 1.2 reshape.34
  41.5 0.0 copy-start.3
  41.5 2.0 %reshape.33 = bf16[128,1536]{1,0:T(8,128)(2,1)} reshape(bf16[32,4,1536]{2,1,0:T(4,128)(2,1)} %get-tuple-element.4) | data formatting | bytes 786432 | tf_op jit(solution)/shard_map/reshape | solution.py:63
  43.5 0.0 copy-done.1
  43.5 1.2 convolution_convert_fusion.6
  44.6 0.0 copy-done.3
  44.6 0.0 copy-done
  44.6 0.0 copy-done.5
  44.7 1.0 convolution_convert_fusion.7
  45.7 0.0 collective-permute-done
  45.7 1.7 %fusion.25 = (bf16[32,4,1536]{2,1,0:T(4,128)(2,1)S(1)}, bf16[32,4,1536]{2,1,0:T(4,128)(2,1)S(1)}) fusion(bf16[32,8,1536]{2,1,0:T(8,128)(2,1)} %collective-permute-done), kind=kLoop, calls=%fused_computation.43 | loop fusion | bytes 1572864 | tf_op jit(solution)/shard_map/slice | solution.py:63
  47.3 0.1 reshape.36
  47.4 0.0 copy-start.7
  47.5 1.2 convolution_convert_fusion.4
  48.6 0.1 reshape.35
  48.7 0.0 copy-done.7
  48.7 0.0 copy-start.9
  48.7 0.0 copy-start.11
  48.7 0.0 copy-start.12
  48.7 0.0 copy-start.13
  48.8 0.4 convolution_convert_fusion.5
  49.1 0.6 copy-done.11
  49.7 0.1 copy-done.12
  49.8 0.0 copy-done.13
  49.9 0.0 copy-done.9
  49.9 22.3 %all_to_all.21 = bf16[8,32,768]{2,1,0:T(8,128)(2,1)S(1)} all-to-all(bf16[8,32,768]{2,1,0:T(8,128)(2,1)S(1)} %bitcast.25), channel_id=1, replica_groups=mesh['row'=8,'col'=8,'x'=4,'core'=2] {'row'}, dimensions={0} | all-to-all | bytes 786432 | tf_op jit(solution)/shard_map/all_to_all | solution.py:43
  72.2 0.1 convert_reduce_fusion
  72.3 17.6 %all_to_all.22 = bf16[8,32,768]{2,1,0:T(8,128)(2,1)S(1)} all-to-all(bf16[8,32,768]{2,1,0:T(8,128)(2,1)S(1)} %broadcast_in_dim.5), channel_id=1, replica_groups=mesh['row'=8,'col'=8,'x'=4,'core'=2] {'row'}, dimensions={0} | all-to-all | bytes 786432 | tf_op jit(solution)/shard_map/all_to_all | solution.py:43
  89.9 0.5 convolution_convert_fusion.2
  90.4 1.1 convolution_convert_fusion.3
  91.5 0.1 stack_reshape.17
  91.6 0.1 copy.15
  91.7 1.1 stack_reshape.16
  92.8 0.1 copy.14
  92.8 0.9 pad_maximum_fusion.1
  93.8 1.9 %collective-permute-start.1 = (bf16[32,8,1536]{2,0,1:T(8,128)(2,1)}, bf16[32,8,1536]{2,0,1:T(8,128)(2,1)}, u32[]{:S(2)}, u32[]{:S(2)}) collective-permute-start(bf16[32,8,1536]{2,0,1:T(8,128)(2,1)} %bitcast.3), channel_id=1, source_target_pairs={{0,1},{1,0},{2,3},{3,2},{4,5},{5,4},{6,7},{7,6},{8,9},{9,8},{10,11... | collective-permute-start | bytes 2359304 | tf_op jit(solution)/shard_map/ppermute | solution.py:39
  95.7 1.4 %fusion.11 = f32[128,1536]{1,0:T(8,128)} fusion(bf16[1536,384]{1,0:T(8,128)(2,1)S(1)} %copy-done, bf16[256,768]{1,0:T(8,128)(2,1)S(1)} %bitcast.21), kind=kOutput, calls=%fused_computation.24 | convolution fusion | flops 150994944 | bytes 2064384 | tf_op jit(solution)/shard_map/dot_general | solution.py:23
  97.1 1.4 %stack_reshape.15 = f32[32,1,4,1536]{3,2,0,1:T(4,128)S(1)} reshape(f32[128,1536]{1,0:T(8,128)} %fusion.11) | data formatting | bytes 1572864 | tf_op jit(solution)/shard_map/stack;reshape | solution.py:86
  98.5 1.1 copy.13
  99.6 0.4 fusion.13
  99.9 0.2 stack_reshape.14
  100.2 0.0 copy-start.2
  100.2 0.3 copy.12
  100.5 0.9 copy-done.2
  101.3 0.1 pad_maximum_fusion
  101.4 0.0 collective-permute-done.1
  101.5 1.4 %fusion = bf16[32,8,1536]{2,0,1:T(8,128)(2,1)S(1)} fusion(f32[32,2,4,1536]{3,0,2,1:T(8,128)S(1)} %pad_maximum_fusion, bf16[32,8,1536]{2,0,1:T(8,128)(2,1)} %collective-permute-done.1), kind=kLoop, calls=%fused_computation.6 | loop fusion | flops 1179648 | bytes 3145728 | tf_op jit(solution)/shard_map/convert_element_type | solution.py:96
  102.9 1.3 copy.16
  104.2 5.7 %all-to-all-start.3 = ((bf16[32,8,1536]{2,1,0:T(8,128)(2,1)}), bf16[32,8,1536]{2,1,0:T(8,128)(2,1)S(1)}, u32[]{:S(2)}, u32[]{:S(2)}) async-start(bf16[32,8,1536]{2,1,0:T(8,128)(2,1)} %copy.16), calls=%async_computation.3 | async-start | bytes 1572864 | tf_op jit(solution)/shard_map/all_to_all | solution.py:43
  109.9 0.0 copy-done.6
  109.9 0.0 copy-done.10
  109.9 0.0 copy-start.4
  109.9 0.0 copy-start.8
  109.9 1.6 %convolution_convert_fusion.1 = bf16[1536,384]{1,0:T(8,128)(2,1)} fusion(bf16[128,1536]{1,0:T(8,128)(2,1)S(1)} %copy-done.10, bf16[128,1536]{1,0:T(8,128)(2,1)S(1)} %copy-done.6, bf16[256,768]{1,0:T(8,128)(2,1)S(1)} %bitcast.23), kind=kOutput, calls=%fused_computation.1 | convolution fusion | flops 304152576 | bytes 2162688 | tf_op jit(solution)/shard_map/dot_general | solution.py:29
  111.6 1.5 %convolution_convert_fusion = bf16[384,1536]{1,0:T(8,128)(2,1)} fusion(bf16[128,1536]{1,0:T(8,128)(2,1)S(1)} %copy-done.8, bf16[128,1536]{1,0:T(8,128)(2,1)S(1)} %copy-done.4, bf16[256,768]{1,0:T(8,128)(2,1)S(1)} %bitcast.24), kind=kOutput, calls=%fused_computation | convolution fusion | flops 304152576 | bytes 2162688 | tf_op jit(solution)/shard_map/dot_general | solution.py:29
  113.1 19.9 %all-to-all-done.3 = bf16[32,8,1536]{2,1,0:T(8,128)(2,1)S(1)} async-done(((bf16[32,8,1536]{2,1,0:T(8,128)(2,1)}), bf16[32,8,1536]{2,1,0:T(8,128)(2,1)S(1)}, u32[]{:S(2)}, u32[]{:S(2)}) %all-to-all-start.3) | async-done | bytes 786464 | tf_op jit(solution)/shard_map/all_to_all | solution.py:43
  133.0 0.1 reduce_sum.22
  133.1 0.6 fusion.26
  (10 shorter events, 0.1 us)
Async XLA Ops:
  0.6 44.0 %copy-start = (bf16[1536,384]{1,0:T(8,128)(2,1)S(1)}, bf16[1536,384]{1,0:T(8,128)(2,1)}, u32[]{:S(2)}) copy-start(bf16[1536,384]{1,0:T(8,128)(2,1)} %param.5) | copy-start | bytes 3538948
  37.3 8.4 %collective-permute-start = (bf16[32,8,1536]{2,1,0:T(8,128)(2,1)S(1)}, bf16[32,8,1536]{2,1,0:T(8,128)(2,1)}, u32[]{:S(2)}, u32[]{:S(2)}) collective-permute-start(bf16[32,8,1536]{2,1,0:T(8,128)(2,1)S(1)} %all_to_all.20), channel_id=1, source_target_pairs={{0,1},{1,0},{2,3},{3,2},{4,5},{5,4},{6,7},{7,6},{8,9},{9,8},{10,11... | collective-permute-start | bytes 2359304 | tf_op jit(solution)/shard_map/ppermute | solution.py:39
  40.3 3.2 %copy-start.1 = (bf16[384,1536]{1,0:T(8,128)(2,1)S(1)}, bf16[384,1536]{1,0:T(8,128)(2,1)}, u32[]{:S(2)}) copy-start(bf16[384,1536]{1,0:T(8,128)(2,1)} %param.6) | copy-start | bytes 3538948
  41.5 3.2 %copy-start.3 = (bf16[128,1536]{1,0:T(8,128)(2,1)}, bf16[128,1536]{1,0:T(8,128)(2,1)S(1)}, u32[]{:S(2)}) copy-start(bf16[128,1536]{1,0:T(8,128)(2,1)S(1)} %reshape.34) | copy-start | bytes 1179652
  43.5 1.2 copy-start.5
  47.4 1.3 copy-start.7
  48.7 1.2 copy-start.9
  48.7 1.0 copy-start.11
  48.7 1.1 copy-start.12
  48.7 1.1 copy-start.13
  93.8 7.7 %collective-permute-start.1 = (bf16[32,8,1536]{2,0,1:T(8,128)(2,1)}, bf16[32,8,1536]{2,0,1:T(8,128)(2,1)}, u32[]{:S(2)}, u32[]{:S(2)}) collective-permute-start(bf16[32,8,1536]{2,0,1:T(8,128)(2,1)} %bitcast.3), channel_id=1, source_target_pairs={{0,1},{1,0},{2,3},{3,2},{4,5},{5,4},{6,7},{7,6},{8,9},{9,8},{10,11... | collective-permute-start | bytes 2359304 | tf_op jit(solution)/shard_map/ppermute | solution.py:39
  100.2 1.1 copy-start.2
  104.2 5.7 %copy-start.6 = (bf16[128,1536]{1,0:T(8,128)(2,1)S(1)}, bf16[128,1536]{1,0:T(8,128)(2,1)}, u32[]{:S(2)}) copy-start(bf16[128,1536]{1,0:T(8,128)(2,1)} %reshape.33) | copy-start | bytes 1179652
  104.2 5.7 %copy-start.10 = (bf16[128,1536]{1,0:T(8,128)(2,1)S(1)}, bf16[128,1536]{1,0:T(8,128)(2,1)}, u32[]{:S(2)}) copy-start(bf16[128,1536]{1,0:T(8,128)(2,1)} %copy-done.9) | copy-start | bytes 1179652
  104.2 28.8 %all-to-all-start.3 = ((bf16[32,8,1536]{2,1,0:T(8,128)(2,1)}), bf16[32,8,1536]{2,1,0:T(8,128)(2,1)S(1)}, u32[]{:S(2)}, u32[]{:S(2)}) async-start(bf16[32,8,1536]{2,1,0:T(8,128)(2,1)} %copy.16), calls=%async_computation.3 | async-start | bytes 1572864 | tf_op jit(solution)/shard_map/all_to_all | solution.py:43
  109.9 1.6 %copy-start.4 = (bf16[128,1536]{1,0:T(8,128)(2,1)S(1)}, bf16[128,1536]{1,0:T(8,128)(2,1)}, u32[]{:S(2)}) copy-start(bf16[128,1536]{1,0:T(8,128)(2,1)} %copy-done.3) | copy-start | bytes 1179652
  109.9 1.6 %copy-start.8 = (bf16[128,1536]{1,0:T(8,128)(2,1)S(1)}, bf16[128,1536]{1,0:T(8,128)(2,1)}, u32[]{:S(2)}) copy-start(bf16[128,1536]{1,0:T(8,128)(2,1)} %copy-done.7) | copy-start | bytes 1179652

commit v2 on v1

v2 whole, which is shorter than its diff:
```python
import math

import jax
import jax.numpy as jnp
from jax import lax
from jax.experimental import pallas as pl
from jax.experimental.pallas import tpu as pltpu
from jax.sharding import Mesh, PartitionSpec as P

root_two_pi = math.sqrt(2.0 / math.pi)
cubic = 0.044715
chips = ("col", "x")
bf16 = jnp.bfloat16
f32 = jnp.float32
mib = 1024 * 1024


def gelu_parts(hidden):
    inner = jnp.tanh(root_two_pi * (hidden + cubic * hidden * hidden * hidden))
    value = 0.5 * hidden * (1.0 + inner)
    slope = 0.5 * (1.0 + inner) + 0.5 * hidden * (1.0 - inner * inner) * root_two_pi * (
        1.0 + 3.0 * cubic * hidden * hidden
    )
    return value, slope


def contract(left, right, left_dim, right_dim):
    return lax.dot_general(
        left, right, (((left_dim,), (right_dim,)), ((), ())), preferred_element_type=f32
    )


def other_core(block):
    return lax.ppermute(block, "core", [(0, 1), (1, 0)])


def exchange(blocks, axes):
    return lax.all_to_all(blocks, axes, split_axis=0, concat_axis=0)


def first_kind(shape, share):
    return lax.broadcasted_iota(jnp.int32, shape, 0) % (2 * share) < share


def whole(kernel, name, out_shapes, args, products, limit=24):
    in_vmem = pl.BlockSpec(memory_space=pltpu.VMEM)
    moved = sum(a.size * a.dtype.itemsize for a in (*args, *jax.tree.leaves(out_shapes)))
    return pl.pallas_call(
        kernel,
        out_shape=out_shapes,
        in_specs=[in_vmem] * len(args),
        out_specs=jax.tree.map(lambda _: in_vmem, out_shapes),
        cost_estimate=pl.CostEstimate(flops=2 * products, bytes_accessed=moved, transcendentals=0),
        compiler_params=pltpu.CompilerParams(vmem_limit_bytes=limit * mib),
        name=name,
    )(*args)


def spread_kernel(tokens_ref, cotangent_ref, out_ref):
    both = jnp.concatenate([tokens_ref[...].astype(f32), cotangent_ref[...].astype(f32)], axis=0)
    both = both.astype(bf16)
    for chip in range(out_ref.shape[0]):
        out_ref[chip] = both


def terms_kernel(share, acts_ref, in_ref, out_ref, in_far_ref, out_far_ref, terms_ref):
    acts = acts_ref[...]
    units = in_ref.shape[1]
    for place, (w_in, w_out) in enumerate(((in_ref, out_ref), (in_far_ref, out_far_ref))):
        value = contract(acts, w_in[...], 1, 0)
        slope = contract(acts, w_out[...], 1, 1)
        picked = jnp.where(first_kind(value.shape, share), value, slope)
        terms_ref[:, place * units : (place + 1) * units] = picked.astype(bf16)


def gelu_kernel(share, terms_ref, out_ref):
    total = terms_ref[0].astype(f32)
    for row in range(1, terms_ref.shape[0]):
        total = total + terms_ref[row].astype(f32)
    first = first_kind(total.shape, share)
    hidden = jnp.where(first, total, pltpu.roll(total, share, 0))
    value, slope = gelu_parts(hidden)
    made = jnp.where(first, value, total * slope).astype(bf16)
    for row in range(out_ref.shape[0]):
        out_ref[row] = made


def sums_kernel(share, made_ref, in_ref, out_ref, in_far_ref, out_far_ref, sums_ref):
    units, width = out_ref.shape
    near, far = made_ref[:, :units], made_ref[:, units:]
    step = 512
    for start in range(0, width, step):
        part = slice(start, start + step)
        ahead = contract(near, out_ref[:, part], 1, 0) + contract(far, out_far_ref[:, part], 1, 0)
        back = contract(near, in_ref[part, :], 1, 1) + contract(far, in_far_ref[part, :], 1, 1)
        picked = jnp.where(first_kind(ahead.shape, share), ahead, back)
        sums_ref[:, part] = picked.astype(bf16)


def weight_kernel(share, acts_ref, acts_far_ref, made_ref, made_far_ref, grad_in_ref, grad_out_ref):
    grads, actives = [], []
    for made in (made_ref, made_far_ref):
        wide = made[...].astype(f32)
        first = first_kind(wide.shape, share)
        up = pltpu.roll(wide, wide.shape[0] - share, 0)
        down = pltpu.roll(wide, share, 0)
        grads.append(jnp.where(first, up, 0.0).astype(bf16))
        actives.append(jnp.where(first, 0.0, down).T.astype(bf16))
    step = 512
    for start in range(0, acts_ref.shape[1], step):
        part = slice(start, start + step)
        near, far = acts_ref[:, part], acts_far_ref[:, part]
        grad_in = contract(near, grads[0], 0, 0) + contract(far, grads[1], 0, 0)
        grad_in_ref[part, :] = grad_in.astype(bf16)
        grad_out = contract(actives[0], near, 1, 0) + contract(actives[1], far, 1, 0)
        grad_out_ref[:, part] = grad_out.astype(bf16)


def bind(kernel, share):
    return lambda *refs: kernel(share, *refs)


def local(tokens, weight_in, weight_out, cotangent):
    rows = lax.axis_size("row")
    count = lax.axis_size("col") * lax.axis_size("x")
    share, width = tokens.shape
    units = weight_in.shape[1]
    held = 2 * share * count
    shaped = lambda *dims: jax.ShapeDtypeStruct(dims, bf16)

    copies = whole(
        spread_kernel, "spread_rows", shaped(count, 2 * share, width), (tokens, cotangent), 0
    )
    weight_in_far = other_core(weight_in)
    weight_out_far = other_core(weight_out)
    weights = (weight_in, weight_out, weight_in_far, weight_out_far)
    acts = exchange(copies, chips).reshape(held, width)

    partial = whole(
        bind(terms_kernel, share),
        "hidden_terms",
        shaped(held, 2 * units),
        (acts, *weights),
        4 * held * width * units,
    )
    received = exchange(partial.reshape(rows, held // rows, 2 * units), "row")
    made = whole(
        bind(gelu_kernel, share), "gelu_rows", shaped(*received.shape), (received,), 0
    )
    made = exchange(made, "row").reshape(held, 2 * units)

    sums = whole(
        bind(sums_kernel, share),
        "output_terms",
        shaped(held, width),
        (made, *weights),
        4 * held * width * units,
    )
    sums, made, acts = lax.optimization_barrier((sums, made, acts))
    blocks = exchange(sums.reshape(count, 2 * share, width), chips)
    final = jnp.sum(blocks.astype(f32), axis=0).astype(bf16)

    made_far = other_core(made[:, units:])
    acts_far = other_core(acts)
    grad_weight_in, grad_weight_out = whole(
        bind(weight_kernel, share),
        "weight_gradients",
        (shaped(width, units), shaped(units, width)),
        (acts, acts_far, made[:, :units], made_far),
        4 * held * width * units,
    )
    return final[:share], final[share:], grad_weight_in, grad_weight_out


def solution(mesh):
    sizes = dict(mesh.shape)
    finer = Mesh(
        mesh.devices.reshape(sizes["row"], sizes["col"], sizes["depth"] // 2, 2),
        ("row", "col", "x", "core"),
    )
    wide = ("col", "x", "core")
    placed = (P(wide, "row"), P("row", wide), P(wide, "row"), P(wide, "row"))
    return jax.shard_map(
        local,
        mesh=finer,
        in_specs=placed,
        out_specs=(P(wide, "row"), P(wide, "row"), P("row", wide), P(wide, "row")),
        check_vma=False,
    )
```

time: 134 us -> 109 us (0.81)
  blocking collectives: 75.5 us -> 34.2 us
  starting transfers between devices: 9.52 us -> 29.8 us
  matrix products: 10.2 us -> 0 us
  Pallas kernels: 0 us -> 9.75 us
  local copies, waits for them, and re-layouts: 14.1 us -> 5.36 us
  waiting for transfers between devices: 19.9 us -> 27.9 us
  other arithmetic: 3.56 us -> 0.12 us
    all_to_all x3 -> x2, blocking collectives: 75.5 us -> 34.2 us  [exchange(): return lax.all_to_all(blocks, axes, split_axis=0, concat_axis=0)]
    all_to_all x1 -> x2, starting transfers between devices: 5.7 us -> 21.2 us  [exchange(): return lax.all_to_all(blocks, axes, split_axis=0, concat_axis=0)]
    dot_general x10 -> x0, matrix products: 10.2 us -> none  [the longest x4 4.18 us: inner_last(): lax.dot_general(left, right, (((1,), (1,)), ((), ())), preferred_element_...]
    pallas_call x0 -> x5, Pallas kernels: none -> 9.75 us  [whole(): pl.pallas_call(kernel, out_shape=out_shapes, in_specs=[in_vmem] * len(arg...]
    ppermute x2 -> x4, starting transfers between devices: 3.82 us -> 8.65 us  [other_core(): return lax.ppermute(block, 'core', [(0, 1), (1, 0)])]
    all_to_all x1 -> x2, waiting for transfers between devices: 19.9 us -> 24.4 us  [exchange(): return lax.all_to_all(blocks, axes, split_axis=0, concat_axis=0)]
    another operation x8 -> x0, local copies, waits for them, and re-layouts: 4.28 us -> none  [products(): jnp.stack([plain(active[rows_of], weight_out).reshape(count, share, width...]
    ppermute x2 -> x4, waiting for transfers between devices: 0.01 us -> 3.5 us  [other_core(): return lax.ppermute(block, 'core', [(0, 1), (1, 0)])]
  transfers between devices with their start and end apart: 3 -> 6, of which waited for: 1 -> 5; matrix products, arithmetic and copies ran while one was open for 11% -> 0% of each run, Pallas kernels for 0% -> 4%
where the time goes in v2:
time: 109 us; the launch traced here: 108 us
  blocking collectives  34.2 us (31%)
  starting transfers between devices  29.8 us (27%)
  waiting for transfers between devices  27.9 us (26%)
  Pallas kernels  9.75 us (9%)
  local copies, waits for them, and re-layouts  5.36 us (5%)
    all_to_all x2, blocking collectives, exchange(): return lax.all_to_all(blocks, axes, split_axis=0, concat_axis=0)  34.2 us
    all_to_all x2, waiting for transfers between devices, exchange(): return lax.all_to_all(blocks, axes, split_axis=0, concat_axis=0)  24.4 us
    all_to_all x2, starting transfers between devices, exchange(): return lax.all_to_all(blocks, axes, split_axis=0, concat_axis=0)  21.2 us
    pallas_call x5, Pallas kernels, whole(): pl.pallas_call(kernel, out_shape=out_shapes, in_specs=[in_vmem] * len(arg...  9.75 us
    ppermute x4, starting transfers between devices, other_core(): return lax.ppermute(block, 'core', [(0, 1), (1, 0)])  8.65 us
    unnamed x18, local copies, waits for them, and re-layouts  4.71 us
    ppermute x4, waiting for transfers between devices, other_core(): return lax.ppermute(block, 'core', [(0, 1), (1, 0)])  3.5 us
  transfers between devices with their start and end apart: 6, of which 5 were waited for; matrix products, arithmetic and copies ran while one was open for 0% of the time, Pallas kernels for 4%

profile of v2, /device:TPU:2, one launch (start us, length us, event | category | flops | bytes accessed | tf_op | source)
XLA Modules:
  0.0 107.9 jit_solution(11585820737664515052)
XLA Ops:
  0.6 0.0 copy-start
  0.6 0.0 copy-start.7
  0.7 0.8 copy-done.7
  1.4 0.0 copy-start.8
  1.4 0.7 copy-done.8
  2.2 0.0 copy-start.1
  2.2 0.9 spread_rows.1
  3.1 13.5 %all-to-all-start = ((bf16[32,8,1536]{2,1,0:T(8,128)(2,1)}), bf16[32,8,1536]{2,1,0:T(8,128)(2,1)}, u32[]{:S(2)}, u32[]{:S(2)}) async-start(bf16[32,8,1536]{2,1,0:T(8,128)(2,1)} %spread_rows.1), calls=%async_computation | async-start | bytes 1572864 | tf_op jit(solution)/shard_map/all_to_all | solution.py:38
  16.6 0.0 copy-done
  16.6 1.9 %collective-permute-start = (bf16[1536,384]{1,0:T(8,128)(2,1)S(1)}, bf16[1536,384]{1,0:T(8,128)(2,1)S(1)}, u32[]{:S(2)}, u32[]{:S(2)}) collective-permute-start(bf16[1536,384]{1,0:T(8,128)(2,1)S(1)} %copy-done), channel_id=1, source_target_pairs={{0,1},{1,0},{2,3},{3,2},{4,5},{5,4},{6,7},{7,6},{8,9},{9,8},{10,11... | collective-permute-start | bytes 3538952 | tf_op jit(solution)/shard_map/ppermute | solution.py:34
  18.5 0.0 copy-done.1
  18.6 2.4 %collective-permute-start.1 = (bf16[384,1536]{1,0:T(8,128)(2,1)S(1)}, bf16[384,1536]{1,0:T(8,128)(2,1)S(1)}, u32[]{:S(2)}, u32[]{:S(2)}) collective-permute-start(bf16[384,1536]{1,0:T(8,128)(2,1)S(1)} %copy-done.1), channel_id=1, source_target_pairs={{0,1},{1,0},{2,3},{3,2},{4,5},{5,4},{6,7},{7,6},{8,9},{9,8},{10,11... | collective-permute-start | bytes 3538952 | tf_op jit(solution)/shard_map/ppermute | solution.py:34
  21.0 0.4 collective-permute-done.refs_3_
  21.4 2.1 %collective-permute-done.1.refs_4_ = bf16[384,1536]{1,0:T(8,128)(2,1)S(1)} collective-permute-done((bf16[384,1536]{1,0:T(8,128)(2,1)S(1)}, bf16[384,1536]{1,0:T(8,128)(2,1)S(1)}, u32[]{:S(2)}, u32[]{:S(2)}) %collective-permute-start.1) | collective-permute-done | bytes 1179680 | tf_op jit(solution)/shard_map/ppermute | solution.py:34
  23.4 0.0 copy-start.2
  23.4 1.0 copy-done.2
  24.4 14.7 %all-to-all-done = bf16[32,8,1536]{2,1,0:T(8,128)(2,1)} async-done(((bf16[32,8,1536]{2,1,0:T(8,128)(2,1)}), bf16[32,8,1536]{2,1,0:T(8,128)(2,1)}, u32[]{:S(2)}, u32[]{:S(2)}) %all-to-all-start) | async-done | bytes 786464 | tf_op jit(solution)/shard_map/all_to_all | solution.py:38
  39.1 0.0 copy-start.3
  39.1 1.3 %copy-done.3 = bf16[384,1536]{1,0:T(8,128)(2,1)S(1)} copy-done((bf16[384,1536]{1,0:T(8,128)(2,1)S(1)}, bf16[384,1536]{1,0:T(8,128)(2,1)}, u32[]{:S(2)}) %copy-start.3) | copy-done | bytes 1179672
  40.4 2.9 %hidden_terms.1 = bf16[256,768]{1,0:T(8,128)(2,1)S(1)} custom-call(bf16[256,1536]{1,0:T(8,128)(2,1)} %bitcast.refs_0_, bf16[1536,384]{1,0:T(8,128)(2,1)S(1)} %copy-done, bf16[384,1536]{1,0:T(8,128)(2,1)S(1)} %copy-done.1, bf16[1536,384]{1,0:T(8,128)(2,1)S(1)} %collective-permute-done.refs_3_, bf16[384,1536]{1,0:T(8,128)(2,1)S(1)} %copy-done.3), custom_call_target="tpu_custom_call" | custom-call | flops 1207959552 | bytes 5898240 | tf_op jit(solution)/shard_map/hidden_terms/pallas_call | solution.py:48
  43.3 19.9 %all_to_all.20.refs_0_ = bf16[8,32,768]{2,1,0:T(8,128)(2,1)S(1)} all-to-all(bf16[8,32,768]{2,1,0:T(8,128)(2,1)S(1)} %bitcast.7), channel_id=1, replica_groups=mesh['row'=8,'col'=8,'x'=4,'core'=2] {'row'}, dimensions={0} | all-to-all | bytes 786432 | tf_op jit(solution)/shard_map/all_to_all | solution.py:38
  63.2 0.1 gelu_rows.1
  63.4 14.3 %all_to_all.21 = bf16[8,32,768]{2,1,0:T(8,128)(2,1)S(1)} all-to-all(bf16[8,32,768]{2,1,0:T(8,128)(2,1)S(1)} %gelu_rows.1), channel_id=1, replica_groups=mesh['row'=8,'col'=8,'x'=4,'core'=2] {'row'}, dimensions={0} | all-to-all | bytes 786432 | tf_op jit(solution)/shard_map/all_to_all | solution.py:38
  77.6 0.0 copy-start.4
  77.6 1.8 %output_terms.1 = bf16[256,1536]{1,0:T(8,128)(2,1)S(1)} custom-call(bf16[256,768]{1,0:T(8,128)(2,1)S(1)} %bitcast.4, bf16[1536,384]{1,0:T(8,128)(2,1)S(1)} %copy-done, bf16[384,1536]{1,0:T(8,128)(2,1)S(1)} %copy-done.1, bf16[1536,384]{1,0:T(8,128)(2,1)S(1)} %collective-permute-done.refs_3_, bf16[384,1536]{1,0:T(8,128)(2,1)S(1)} %copy-done.3), custom_call_target="tpu_custom_call" | custom-call | flops 1207959552 | bytes 5898240 | tf_op jit(solution)/shard_map/output_terms/pallas_call | solution.py:48
  79.4 0.0 copy-done.4
  79.5 0.0 copy-start.6
  79.5 0.9 copy-done.6
  80.4 0.0 copy-start.5
  80.4 7.6 %all-to-all-start.3 = ((bf16[32,8,1536]{2,1,0:T(8,128)(2,1)}), bf16[32,8,1536]{2,1,0:T(8,128)(2,1)S(1)}, u32[]{:S(2)}, u32[]{:S(2)}) async-start(bf16[32,8,1536]{2,1,0:T(8,128)(2,1)} %bitcast.6), calls=%async_computation.3 | async-start | bytes 1572864 | tf_op jit(solution)/shard_map/all_to_all | solution.py:38
  88.0 1.9 %collective-permute-start.2 = (bf16[256,1536]{1,0:T(8,128)(2,1)}, bf16[256,1536]{1,0:T(8,128)(2,1)S(1)}, u32[]{:S(2)}, u32[]{:S(2)}) collective-permute-start(bf16[256,1536]{1,0:T(8,128)(2,1)} %bitcast.refs_0_), channel_id=1, source_target_pairs={{0,1},{1,0},{2,3},{3,2},{4,5},{5,4},{6,7},{7,6},{8,9},{9,8},{10,11... | collective-permute-start | bytes 2359304 | tf_op jit(solution)/shard_map/ppermute | solution.py:34
  89.9 0.0 copy-done.5
  90.0 2.4 %collective-permute-start.3 = (bf16[256,384]{1,0:T(8,128)(2,1)S(1)}, bf16[256,384]{1,0:T(8,128)(2,1)S(1)}, u32[]{:S(2)}, u32[]{:S(2)}) collective-permute-start(bf16[256,384]{1,0:T(8,128)(2,1)S(1)} %get-tuple-element.14), channel_id=1, source_target_pairs={{0,1},{1,0},{2,3},{3,2},{4,5},{5,4},{6,7},{7,6},{8,9},{9,8},{10,11... | collective-permute-start | bytes 589832 | tf_op jit(solution)/shard_map/ppermute | solution.py:34
  92.4 1.0 collective-permute-done.3.refs_3_
  93.5 0.0 collective-permute-done.2.refs_1_
  93.5 4.0 %weight_gradients.1 = (bf16[1536,384]{1,0:T(8,128)(2,1)}, bf16[384,1536]{1,0:T(8,128)(2,1)}) custom-call(bf16[256,1536]{1,0:T(8,128)(2,1)} %bitcast.refs_0_, bf16[256,1536]{1,0:T(8,128)(2,1)S(1)} %collective-permute-done.2.refs_1_, bf16[256,384]{1,0:T(8,128)(2,1)S(1)} %get-tuple-element.15.refs_2_, bf16[256,384]{1,0:T(8,128)(2,1)S(1)} %collective-permute-done.3.refs_3_), custom_call_target="tpu_custom_call" | custom-call | flops 1207959552 | bytes 4325376 | tf_op jit(solution)/shard_map/weight_gradients/pallas_call | solution.py:48
  97.4 9.7 %all-to-all-done.3 = bf16[32,8,1536]{2,1,0:T(8,128)(2,1)S(1)} async-done(((bf16[32,8,1536]{2,1,0:T(8,128)(2,1)}), bf16[32,8,1536]{2,1,0:T(8,128)(2,1)S(1)}, u32[]{:S(2)}, u32[]{:S(2)}) %all-to-all-start.3) | async-done | bytes 786464 | tf_op jit(solution)/shard_map/all_to_all | solution.py:38
  107.1 0.1 reduce_sum.12
  107.2 0.6 fusion.1
  (1 shorter events, 0.0 us)
Async XLA Ops:
  0.6 16.0 %copy-start = (bf16[1536,384]{1,0:T(8,128)(2,1)S(1)}, bf16[1536,384]{1,0:T(8,128)(2,1)}, u32[]{:S(2)}) copy-start(bf16[1536,384]{1,0:T(8,128)(2,1)} %refs_1_.3) | copy-start | bytes 3538948
  0.6 0.8 copy-start.7
  1.4 0.7 copy-start.8
  2.2 16.4 %copy-start.1 = (bf16[384,1536]{1,0:T(8,128)(2,1)S(1)}, bf16[384,1536]{1,0:T(8,128)(2,1)}, u32[]{:S(2)}) copy-start(bf16[384,1536]{1,0:T(8,128)(2,1)} %refs_2_.3) | copy-start | bytes 3538948
  3.1 36.0 %all-to-all-start = ((bf16[32,8,1536]{2,1,0:T(8,128)(2,1)}), bf16[32,8,1536]{2,1,0:T(8,128)(2,1)}, u32[]{:S(2)}, u32[]{:S(2)}) async-start(bf16[32,8,1536]{2,1,0:T(8,128)(2,1)} %spread_rows.1), calls=%async_computation | async-start | bytes 1572864 | tf_op jit(solution)/shard_map/all_to_all | solution.py:38
  16.6 4.7 %collective-permute-start = (bf16[1536,384]{1,0:T(8,128)(2,1)S(1)}, bf16[1536,384]{1,0:T(8,128)(2,1)S(1)}, u32[]{:S(2)}, u32[]{:S(2)}) collective-permute-start(bf16[1536,384]{1,0:T(8,128)(2,1)S(1)} %copy-done), channel_id=1, source_target_pairs={{0,1},{1,0},{2,3},{3,2},{4,5},{5,4},{6,7},{7,6},{8,9},{9,8},{10,11... | collective-permute-start | bytes 3538952 | tf_op jit(solution)/shard_map/ppermute | solution.py:34
  18.6 4.9 %collective-permute-start.1 = (bf16[384,1536]{1,0:T(8,128)(2,1)S(1)}, bf16[384,1536]{1,0:T(8,128)(2,1)S(1)}, u32[]{:S(2)}, u32[]{:S(2)}) collective-permute-start(bf16[384,1536]{1,0:T(8,128)(2,1)S(1)} %copy-done.1), channel_id=1, source_target_pairs={{0,1},{1,0},{2,3},{3,2},{4,5},{5,4},{6,7},{7,6},{8,9},{9,8},{10,11... | collective-permute-start | bytes 3538952 | tf_op jit(solution)/shard_map/ppermute | solution.py:34
  23.4 1.0 copy-start.2
  39.1 1.3 %copy-start.3 = (bf16[384,1536]{1,0:T(8,128)(2,1)S(1)}, bf16[384,1536]{1,0:T(8,128)(2,1)}, u32[]{:S(2)}) copy-start(bf16[384,1536]{1,0:T(8,128)(2,1)} %copy-done.2) | copy-start | bytes 3538948
  77.6 1.8 %copy-start.4 = (bf16[8,32,768]{2,1,0:T(8,128)(2,1)}, bf16[8,32,768]{2,1,0:T(8,128)(2,1)S(1)}, u32[]{:S(2)}) copy-start(bf16[8,32,768]{2,1,0:T(8,128)(2,1)S(1)} %all_to_all.21) | copy-start | bytes 1179652
  79.5 0.9 copy-start.6
  80.4 9.6 %copy-start.5 = (bf16[8,32,768]{2,1,0:T(8,128)(2,1)S(1)}, bf16[8,32,768]{2,1,0:T(8,128)(2,1)}, u32[]{:S(2)}) copy-start(bf16[8,32,768]{2,1,0:T(8,128)(2,1)} %copy-done.4) | copy-start | bytes 1179652
  80.4 26.8 %all-to-all-start.3 = ((bf16[32,8,1536]{2,1,0:T(8,128)(2,1)}), bf16[32,8,1536]{2,1,0:T(8,128)(2,1)S(1)}, u32[]{:S(2)}, u32[]{:S(2)}) async-start(bf16[32,8,1536]{2,1,0:T(8,128)(2,1)} %bitcast.6), calls=%async_computation.3 | async-start | bytes 1572864 | tf_op jit(solution)/shard_map/all_to_all | solution.py:38
  88.0 5.5 %collective-permute-start.2 = (bf16[256,1536]{1,0:T(8,128)(2,1)}, bf16[256,1536]{1,0:T(8,128)(2,1)S(1)}, u32[]{:S(2)}, u32[]{:S(2)}) collective-permute-start(bf16[256,1536]{1,0:T(8,128)(2,1)} %bitcast.refs_0_), channel_id=1, source_target_pairs={{0,1},{1,0},{2,3},{3,2},{4,5},{5,4},{6,7},{7,6},{8,9},{9,8},{10,11... | collective-permute-start | bytes 2359304 | tf_op jit(solution)/shard_map/ppermute | solution.py:34
  90.0 3.5 %collective-permute-start.3 = (bf16[256,384]{1,0:T(8,128)(2,1)S(1)}, bf16[256,384]{1,0:T(8,128)(2,1)S(1)}, u32[]{:S(2)}, u32[]{:S(2)}) collective-permute-start(bf16[256,384]{1,0:T(8,128)(2,1)S(1)} %get-tuple-element.14), channel_id=1, source_target_pairs={{0,1},{1,0},{2,3},{3,2},{4,5},{5,4},{6,7},{7,6},{8,9},{9,8},{10,11... | collective-permute-start | bytes 589832 | tf_op jit(solution)/shard_map/ppermute | solution.py:34

commit v3 on v2

--- a/solution.py
+++ b/solution.py
@@ -42,35 +42,47 @@
     return lax.broadcasted_iota(jnp.int32, shape, 0) % (2 * share) < share
 
 
-def whole(kernel, name, out_shapes, args, products, limit=24):
+def whole(kernel, name, out_shapes, args, products, far=0, out_far=0, scratch=(), limit=24):
     in_vmem = pl.BlockSpec(memory_space=pltpu.VMEM)
+    in_hbm = pl.BlockSpec(memory_space=pltpu.HBM)
     moved = sum(a.size * a.dtype.itemsize for a in (*args, *jax.tree.leaves(out_shapes)))
     return pl.pallas_call(
         kernel,
         out_shape=out_shapes,
-        in_specs=[in_vmem] * len(args),
-        out_specs=jax.tree.map(lambda _: in_vmem, out_shapes),
+        in_specs=[in_vmem] * (len(args) - far) + [in_hbm] * far,
+        out_specs=[in_vmem] * (len(out_shapes) - out_far) + [in_hbm] * out_far,
+        scratch_shapes=list(scratch),
         cost_estimate=pl.CostEstimate(flops=2 * products, bytes_accessed=moved, transcendentals=0),
         compiler_params=pltpu.CompilerParams(vmem_limit_bytes=limit * mib),
         name=name,
     )(*args)
 
 
-def spread_kernel(tokens_ref, cotangent_ref, out_ref):
-    both = jnp.concatenate([tokens_ref[...].astype(f32), cotangent_ref[...].astype(f32)], axis=0)
-    both = both.astype(bf16)
-    for chip in range(out_ref.shape[0]):
-        out_ref[chip] = both
-
-
-def terms_kernel(share, acts_ref, in_ref, out_ref, in_far_ref, out_far_ref, terms_ref):
+def terms_kernel(share, acts_hbm, *refs):
+    weights_hbm, terms_ref, kept_hbm, acts_ref, weights, sems = (
+        refs[:4], refs[4], refs[5], refs[6], refs[7:11], refs[11]
+    )
+    fetches = [
+        pltpu.make_async_copy(source, target, sems.at[place])
+        for place, (source, target) in enumerate(
+            zip((acts_hbm, *weights_hbm), (acts_ref, *weights))
+        )
+    ]
+    for fetch in fetches:
+        fetch.start()
+    units = weights[0].shape[1]
+    fetches[0].wait()
+    keep = pltpu.make_async_copy(acts_ref, kept_hbm, sems.at[len(fetches)])
+    keep.start()
     acts = acts_ref[...]
-    units = in_ref.shape[1]
-    for place, (w_in, w_out) in enumerate(((in_ref, out_ref), (in_far_ref, out_far_ref))):
-        value = contract(acts, w_in[...], 1, 0)
-        slope = contract(acts, w_out[...], 1, 1)
+    for side in range(2):
+        fetches[1 + 2 * side].wait()
+        value = contract(acts, weights[2 * side][...], 1, 0)
+        fetches[2 + 2 * side].wait()
+        slope = contract(acts, weights[2 * side + 1][...], 1, 1)
         picked = jnp.where(first_kind(value.shape, share), value, slope)
-        terms_ref[:, place * units : (place + 1) * units] = picked.astype(bf16)
+        terms_ref[:, side * units : (side + 1) * units] = picked.astype(bf16)
+    keep.wait()
 
 
 def gelu_kernel(share, terms_ref, out_ref):
@@ -85,16 +97,39 @@
         out_ref[row] = made
 
 
-def sums_kernel(share, made_ref, in_ref, out_ref, in_far_ref, out_far_ref, sums_ref):
-    units, width = out_ref.shape
+def sums_kernel(share, made_hbm, *refs):
+    weights_hbm, sums_hbm, made_ref, weights, sums_ref, sems = (
+        refs[:4], refs[4], refs[5], refs[6:10], refs[10], refs[11]
+    )
+    units, width = weights[1].shape
+    step = 512
+    parts = [slice(start, start + step) for start in range(0, width, step)]
+    fetch_made = pltpu.make_async_copy(made_hbm, made_ref, sems.at[0, len(parts)])
+    fetch_made.start()
+    fetches, stores = [], []
+    for place, part in enumerate(parts):
+        fetches.append([])
+        for kind, (source, target) in enumerate(zip(weights_hbm, weights)):
+            cut = (part, slice(None)) if kind % 2 == 0 else (slice(None), part)
+            fetch = pltpu.make_async_copy(source.at[cut], target.at[cut], sems.at[kind, place])
+            fetch.start()
+            fetches[-1].append(fetch)
+        stores.append(
+            pltpu.make_async_copy(sums_ref.at[:, part], sums_hbm.at[:, part], sems.at[4, place])
+        )
+    in_near, out_near, in_far, out_far = weights
+    fetch_made.wait()
     near, far = made_ref[:, :units], made_ref[:, units:]
-    step = 512
-    for start in range(0, width, step):
-        part = slice(start, start + step)
-        ahead = contract(near, out_ref[:, part], 1, 0) + contract(far, out_far_ref[:, part], 1, 0)
-        back = contract(near, in_ref[part, :], 1, 1) + contract(far, in_far_ref[part, :], 1, 1)
+    for part, ready, store in zip(parts, fetches, stores):
+        for fetch in ready:
+            fetch.wait()
+        ahead = contract(near, out_near[:, part], 1, 0) + contract(far, out_far[:, part], 1, 0)
+        back = contract(near, in_near[part, :], 1, 1) + contract(far, in_far[part, :], 1, 1)
         picked = jnp.where(first_kind(ahead.shape, share), ahead, back)
         sums_ref[:, part] = picked.astype(bf16)
+        store.start()
+    for store in stores:
+        store.wait()
 
 
 def weight_kernel(share, acts_ref, acts_far_ref, made_ref, made_far_ref, grad_in_ref, grad_out_ref):
@@ -128,33 +163,46 @@
     held = 2 * share * count
     shaped = lambda *dims: jax.ShapeDtypeStruct(dims, bf16)
 
-    copies = whole(
-        spread_kernel, "spread_rows", shaped(count, 2 * share, width), (tokens, cotangent), 0
-    )
+    both = jnp.concatenate([tokens, cotangent], axis=0)
+    copies = jnp.broadcast_to(both[None], (count,) + both.shape)
     weight_in_far = other_core(weight_in)
     weight_out_far = other_core(weight_out)
     weights = (weight_in, weight_out, weight_in_far, weight_out_far)
+    held_weights = [pltpu.VMEM(w.shape, bf16) for w in weights]
     acts = exchange(copies, chips).reshape(held, width)
 
-    partial = whole(
+    partial, acts = whole(
         bind(terms_kernel, share),
         "hidden_terms",
-        shaped(held, 2 * units),
+        [shaped(held, 2 * units), shaped(held, width)],
         (acts, *weights),
         4 * held * width * units,
+        far=5,
+        out_far=1,
+        scratch=(pltpu.VMEM(acts.shape, bf16), *held_weights, pltpu.SemaphoreType.DMA((6,))),
+        limit=60,
     )
     received = exchange(partial.reshape(rows, held // rows, 2 * units), "row")
-    made = whole(
-        bind(gelu_kernel, share), "gelu_rows", shaped(*received.shape), (received,), 0
+    (made,) = whole(
+        bind(gelu_kernel, share), "gelu_rows", [shaped(*received.shape)], (received,), 0
     )
     made = exchange(made, "row").reshape(held, 2 * units)
 
-    sums = whole(
+    (sums,) = whole(
         bind(sums_kernel, share),
         "output_terms",
-        shaped(held, width),
+        [shaped(held, width)],
         (made, *weights),
         4 * held * width * units,
+        far=5,
+        out_far=1,
+        scratch=(
+            pltpu.VMEM(made.shape, bf16),
+            *held_weights,
+            pltpu.VMEM((held, width), bf16),
+            pltpu.SemaphoreType.DMA((5, width // 512 + 1)),
+        ),
+        limit=60,
     )
     sums, made, acts = lax.optimization_barrier((sums, made, acts))
     blocks = exchange(sums.reshape(count, 2 * share, width), chips)
@@ -165,7 +213,7 @@
     grad_weight_in, grad_weight_out = whole(
         bind(weight_kernel, share),
         "weight_gradients",
-        (shaped(width, units), shaped(units, width)),
+        [shaped(width, units), shaped(units, width)],
         (acts, acts_far, made[:, :units], made_far),
         4 * held * width * units,
     )

time: 109 us -> 111 us (1.018)
  local copies, waits for them, and re-layouts: 5.36 us -> 1.62 us
  Pallas kernels: 9.75 us -> 12.2 us
  waiting for transfers between devices: 27.9 us -> 30 us
    unnamed x18 -> x10, local copies, waits for them, and re-layouts: 4.71 us -> 0.03 us
    pallas_call x5 -> x4, Pallas kernels: 9.75 us -> 12.2 us  [whole(): pl.pallas_call(kernel, out_shape=out_shapes, in_specs=[in_vmem] * (len(ar...]
    all_to_all x2, waiting for transfers between devices: 24.4 us -> 26.4 us  [exchange(): return lax.all_to_all(blocks, axes, split_axis=0, concat_axis=0)]
  transfers between devices with their start and end apart: 6 -> 6, of which waited for: 5 -> 5; matrix products, arithmetic and copies ran while one was open for 0% -> 0% of each run, Pallas kernels for 4% -> 3%
where the time goes in v3:
time: 111 us; the launch traced here: 110 us
  blocking collectives  35.1 us (32%)
  starting transfers between devices  30 us (27%)
  waiting for transfers between devices  30 us (27%)
  Pallas kernels  12.2 us (11%)
  local copies, waits for them, and re-layouts  1.62 us (1%)
    all_to_all x2, blocking collectives, exchange(): return lax.all_to_all(blocks, axes, split_axis=0, concat_axis=0)  35.1 us
    all_to_all x2, waiting for transfers between devices, exchange(): return lax.all_to_all(blocks, axes, split_axis=0, concat_axis=0)  26.4 us
    all_to_all x2, starting transfers between devices, exchange(): return lax.all_to_all(blocks, axes, split_axis=0, concat_axis=0)  21.3 us
    pallas_call x4, Pallas kernels, whole(): pl.pallas_call(kernel, out_shape=out_shapes, in_specs=[in_vmem] * (len(ar...  12.2 us
    ppermute x4, starting transfers between devices, other_core(): return lax.ppermute(block, 'core', [(0, 1), (1, 0)])  8.65 us
    ppermute x4, waiting for transfers between devices, other_core(): return lax.ppermute(block, 'core', [(0, 1), (1, 0)])  3.63 us
  transfers between devices with their start and end apart: 6, of which 5 were waited for; matrix products, arithmetic and copies ran while one was open for 0% of the time, Pallas kernels for 3%

profile of v3, /device:TPU:2, one launch (start us, length us, event | category | flops | bytes accessed | tf_op | source)
XLA Modules:
  0.0 110.5 jit_solution(577981344210432031)
XLA Ops:
  0.6 0.7 pad_maximum_fusion
  1.4 0.0 copy-start.1
  1.4 0.0 copy-start.2
  1.4 0.9 broadcast_in_dim.2
  2.3 13.6 %all-to-all-start = ((bf16[32,8,1536]{2,1,0:T(8,128)(2,1)}), bf16[32,8,1536]{2,1,0:T(8,128)(2,1)}, u32[]{:S(2)}, u32[]{:S(2)}) async-start(bf16[32,8,1536]{2,1,0:T(8,128)(2,1)} %broadcast_in_dim.2), calls=%async_computation | async-start | bytes 1572864 | tf_op jit(solution)/shard_map/all_to_all | solution.py:38
  16.0 0.0 copy-done.1
  16.0 1.9 %collective-permute-start = (bf16[1536,384]{1,0:T(8,128)(2,1)S(1)}, bf16[1536,384]{1,0:T(8,128)(2,1)S(1)}, u32[]{:S(2)}, u32[]{:S(2)}) collective-permute-start(bf16[1536,384]{1,0:T(8,128)(2,1)S(1)} %copy-done.1), channel_id=1, source_target_pairs={{0,1},{1,0},{2,3},{3,2},{4,5},{5,4},{6,7},{7,6},{8,9},{9,8},{10,11... | collective-permute-start | bytes 3538952 | tf_op jit(solution)/shard_map/ppermute | solution.py:34
  17.9 0.0 copy-done.2
  17.9 2.4 %collective-permute-start.1 = (bf16[384,1536]{1,0:T(8,128)(2,1)S(1)}, bf16[384,1536]{1,0:T(8,128)(2,1)}, u32[]{:S(2)}, u32[]{:S(2)}) collective-permute-start(bf16[384,1536]{1,0:T(8,128)(2,1)S(1)} %copy-done.2), channel_id=1, source_target_pairs={{0,1},{1,0},{2,3},{3,2},{4,5},{5,4},{6,7},{7,6},{8,9},{9,8},{10,11... | collective-permute-start | bytes 3538952 | tf_op jit(solution)/shard_map/ppermute | solution.py:34
  20.3 0.4 collective-permute-done.refs_3_
  20.7 0.0 copy-start.3
  20.7 2.2 %collective-permute-done.1.refs_4_ = bf16[384,1536]{1,0:T(8,128)(2,1)} collective-permute-done((bf16[384,1536]{1,0:T(8,128)(2,1)S(1)}, bf16[384,1536]{1,0:T(8,128)(2,1)}, u32[]{:S(2)}, u32[]{:S(2)}) %collective-permute-start.1) | collective-permute-done | bytes 1179680 | tf_op jit(solution)/shard_map/ppermute | solution.py:34
  22.9 15.6 %all-to-all-done = bf16[32,8,1536]{2,1,0:T(8,128)(2,1)} async-done(((bf16[32,8,1536]{2,1,0:T(8,128)(2,1)}), bf16[32,8,1536]{2,1,0:T(8,128)(2,1)}, u32[]{:S(2)}, u32[]{:S(2)}) %all-to-all-start) | async-done | bytes 786464 | tf_op jit(solution)/shard_map/all_to_all | solution.py:38
  38.5 0.0 copy-done.3
  38.5 4.7 %hidden_terms.1 = (bf16[256,768]{1,0:T(8,128)(2,1)}, bf16[256,1536]{1,0:T(8,128)(2,1)}) custom-call(bf16[256,1536]{1,0:T(8,128)(2,1)} %bitcast.refs_0_, bf16[1536,384]{1,0:T(8,128)(2,1)} %refs_1_.3, bf16[384,1536]{1,0:T(8,128)(2,1)} %refs_2_.3, bf16[1536,384]{1,0:T(8,128)(2,1)} %copy-done.3, bf16[384,1536]{1,0:T(8,128)(2,1)} %collective-permute-done.1.refs_4_), custom_call_target="tpu_custom_call" | custom-call | flops 1207959552 | bytes 6684672 | tf_op jit(solution)/shard_map/hidden_terms/pallas_call | solution.py:49
  43.2 20.1 %all_to_all.20.refs_0_ = bf16[8,32,768]{2,1,0:T(8,128)(2,1)S(1)} all-to-all(bf16[8,32,768]{2,1,0:T(8,128)(2,1)} %bitcast.7), channel_id=1, replica_groups=mesh['row'=8,'col'=8,'x'=4,'core'=2] {'row'}, dimensions={0} | all-to-all | bytes 786432 | tf_op jit(solution)/shard_map/all_to_all | solution.py:38
  63.3 0.1 gelu_rows.1
  63.4 15.0 %all_to_all.21 = bf16[8,32,768]{2,1,0:T(8,128)(2,1)} all-to-all(bf16[8,32,768]{2,1,0:T(8,128)(2,1)S(1)} %gelu_rows.1), channel_id=1, replica_groups=mesh['row'=8,'col'=8,'x'=4,'core'=2] {'row'}, dimensions={0} | all-to-all | bytes 786432 | tf_op jit(solution)/shard_map/all_to_all | solution.py:38
  78.4 4.5 %output_terms.1 = bf16[256,1536]{1,0:T(8,128)(2,1)} custom-call(bf16[256,768]{1,0:T(8,128)(2,1)} %bitcast.4, bf16[1536,384]{1,0:T(8,128)(2,1)} %refs_1_.3, bf16[384,1536]{1,0:T(8,128)(2,1)} %refs_2_.3, bf16[1536,384]{1,0:T(8,128)(2,1)} %copy-done.3, bf16[384,1536]{1,0:T(8,128)(2,1)} %collective-permute-done.1.refs_4_), custom_call_target="tpu_custom_call" | custom-call | flops 1207959552 | bytes 5898240 | tf_op jit(solution)/shard_map/output_terms/pallas_call | solution.py:49
  82.9 0.0 copy-start
  82.9 0.0 copy-start.4
  82.9 7.7 %all-to-all-start.3 = ((bf16[32,8,1536]{2,1,0:T(8,128)(2,1)}), bf16[32,8,1536]{2,1,0:T(8,128)(2,1)S(1)}, u32[]{:S(2)}, u32[]{:S(2)}) async-start(bf16[32,8,1536]{2,1,0:T(8,128)(2,1)} %bitcast.6), calls=%async_computation.3 | async-start | bytes 1572864 | tf_op jit(solution)/shard_map/all_to_all | solution.py:38
  90.6 0.0 copy-done
  90.6 1.9 %collective-permute-start.2 = (bf16[256,1536]{1,0:T(8,128)(2,1)S(1)}, bf16[256,1536]{1,0:T(8,128)(2,1)S(1)}, u32[]{:S(2)}, u32[]{:S(2)}) collective-permute-start(bf16[256,1536]{1,0:T(8,128)(2,1)S(1)} %copy-done), channel_id=1, source_target_pairs={{0,1},{1,0},{2,3},{3,2},{4,5},{5,4},{6,7},{7,6},{8,9},{9,8},{10,11... | collective-permute-start | bytes 2359304 | tf_op jit(solution)/shard_map/ppermute | solution.py:34
  92.5 0.0 copy-done.4
  92.6 2.4 %collective-permute-start.3 = (bf16[256,384]{1,0:T(8,128)(2,1)S(1)}, bf16[256,384]{1,0:T(8,128)(2,1)S(1)}, u32[]{:S(2)}, u32[]{:S(2)}) collective-permute-start(bf16[256,384]{1,0:T(8,128)(2,1)S(1)} %get-tuple-element.18), channel_id=1, source_target_pairs={{0,1},{1,0},{2,3},{3,2},{4,5},{5,4},{6,7},{7,6},{8,9},{9,8},{10,11... | collective-permute-start | bytes 589832 | tf_op jit(solution)/shard_map/ppermute | solution.py:34
  95.0 1.0 collective-permute-done.3.refs_3_
  96.1 0.0 collective-permute-done.2.refs_1_
  96.1 2.8 %weight_gradients.1 = (bf16[1536,384]{1,0:T(8,128)(2,1)}, bf16[384,1536]{1,0:T(8,128)(2,1)}) custom-call(bf16[256,1536]{1,0:T(8,128)(2,1)S(1)} %copy-done, bf16[256,1536]{1,0:T(8,128)(2,1)S(1)} %collective-permute-done.2.refs_1_, bf16[256,384]{1,0:T(8,128)(2,1)S(1)} %get-tuple-element.19.refs_2_, bf16[256,384]{1,0:T(8,128)(2,1)S(1)} %collective-permute-done.3.refs_3_), custom_call_target="tpu_custom_call" | custom-call | flops 1207959552 | bytes 4325376 | tf_op jit(solution)/shard_map/weight_gradients/pallas_call | solution.py:49
  98.9 10.8 %all-to-all-done.3 = bf16[32,8,1536]{2,1,0:T(8,128)(2,1)S(1)} async-done(((bf16[32,8,1536]{2,1,0:T(8,128)(2,1)}), bf16[32,8,1536]{2,1,0:T(8,128)(2,1)S(1)}, u32[]{:S(2)}, u32[]{:S(2)}) %all-to-all-start.3) | async-done | bytes 786464 | tf_op jit(solution)/shard_map/all_to_all | solution.py:38
  109.7 0.1 reduce_sum.12
  109.8 0.6 fusion.1
  (1 shorter events, 0.0 us)
Async XLA Ops:
  1.4 14.6 %copy-start.1 = (bf16[1536,384]{1,0:T(8,128)(2,1)S(1)}, bf16[1536,384]{1,0:T(8,128)(2,1)}, u32[]{:S(2)}) copy-start(bf16[1536,384]{1,0:T(8,128)(2,1)} %refs_1_.3) | copy-start | bytes 3538948
  1.4 16.5 %copy-start.2 = (bf16[384,1536]{1,0:T(8,128)(2,1)S(1)}, bf16[384,1536]{1,0:T(8,128)(2,1)}, u32[]{:S(2)}) copy-start(bf16[384,1536]{1,0:T(8,128)(2,1)} %refs_2_.3) | copy-start | bytes 3538948
  2.3 36.2 %all-to-all-start = ((bf16[32,8,1536]{2,1,0:T(8,128)(2,1)}), bf16[32,8,1536]{2,1,0:T(8,128)(2,1)}, u32[]{:S(2)}, u32[]{:S(2)}) async-start(bf16[32,8,1536]{2,1,0:T(8,128)(2,1)} %broadcast_in_dim.2), calls=%async_computation | async-start | bytes 1572864 | tf_op jit(solution)/shard_map/all_to_all | solution.py:38
  16.0 4.7 %collective-permute-start = (bf16[1536,384]{1,0:T(8,128)(2,1)S(1)}, bf16[1536,384]{1,0:T(8,128)(2,1)S(1)}, u32[]{:S(2)}, u32[]{:S(2)}) collective-permute-start(bf16[1536,384]{1,0:T(8,128)(2,1)S(1)} %copy-done.1), channel_id=1, source_target_pairs={{0,1},{1,0},{2,3},{3,2},{4,5},{5,4},{6,7},{7,6},{8,9},{9,8},{10,11... | collective-permute-start | bytes 3538952 | tf_op jit(solution)/shard_map/ppermute | solution.py:34
  17.9 5.0 %collective-permute-start.1 = (bf16[384,1536]{1,0:T(8,128)(2,1)S(1)}, bf16[384,1536]{1,0:T(8,128)(2,1)}, u32[]{:S(2)}, u32[]{:S(2)}) collective-permute-start(bf16[384,1536]{1,0:T(8,128)(2,1)S(1)} %copy-done.2), channel_id=1, source_target_pairs={{0,1},{1,0},{2,3},{3,2},{4,5},{5,4},{6,7},{7,6},{8,9},{9,8},{10,11... | collective-permute-start | bytes 3538952 | tf_op jit(solution)/shard_map/ppermute | solution.py:34
  20.7 17.8 %copy-start.3 = (bf16[1536,384]{1,0:T(8,128)(2,1)}, bf16[1536,384]{1,0:T(8,128)(2,1)S(1)}, u32[]{:S(2)}) copy-start(bf16[1536,384]{1,0:T(8,128)(2,1)S(1)} %collective-permute-done.refs_3_) | copy-start | bytes 3538948
  82.9 7.7 %copy-start = (bf16[256,1536]{1,0:T(8,128)(2,1)S(1)}, bf16[256,1536]{1,0:T(8,128)(2,1)}, u32[]{:S(2)}) copy-start(bf16[256,1536]{1,0:T(8,128)(2,1)} %get-tuple-element.14.refs_0_) | copy-start | bytes 2359300
  82.9 9.6 %copy-start.4 = (bf16[8,32,768]{2,1,0:T(8,128)(2,1)S(1)}, bf16[8,32,768]{2,1,0:T(8,128)(2,1)}, u32[]{:S(2)}) copy-start(bf16[8,32,768]{2,1,0:T(8,128)(2,1)} %all_to_all.21) | copy-start | bytes 1179652
  82.9 26.8 %all-to-all-start.3 = ((bf16[32,8,1536]{2,1,0:T(8,128)(2,1)}), bf16[32,8,1536]{2,1,0:T(8,128)(2,1)S(1)}, u32[]{:S(2)}, u32[]{:S(2)}) async-start(bf16[32,8,1536]{2,1,0:T(8,128)(2,1)} %bitcast.6), calls=%async_computation.3 | async-start | bytes 1572864 | tf_op jit(solution)/shard_map/all_to_all | solution.py:38
  90.6 5.5 %collective-permute-start.2 = (bf16[256,1536]{1,0:T(8,128)(2,1)S(1)}, bf16[256,1536]{1,0:T(8,128)(2,1)S(1)}, u32[]{:S(2)}, u32[]{:S(2)}) collective-permute-start(bf16[256,1536]{1,0:T(8,128)(2,1)S(1)} %copy-done), channel_id=1, source_target_pairs={{0,1},{1,0},{2,3},{3,2},{4,5},{5,4},{6,7},{7,6},{8,9},{9,8},{10,11... | collective-permute-start | bytes 2359304 | tf_op jit(solution)/shard_map/ppermute | solution.py:34
  92.6 3.5 %collective-permute-start.3 = (bf16[256,384]{1,0:T(8,128)(2,1)S(1)}, bf16[256,384]{1,0:T(8,128)(2,1)S(1)}, u32[]{:S(2)}, u32[]{:S(2)}) collective-permute-start(bf16[256,384]{1,0:T(8,128)(2,1)S(1)} %get-tuple-element.18), channel_id=1, source_target_pairs={{0,1},{1,0},{2,3},{3,2},{4,5},{5,4},{6,7},{7,6},{8,9},{9,8},{10,11... | collective-permute-start | bytes 589832 | tf_op jit(solution)/shard_map/ppermute | solution.py:34

commit v4 on v2

--- a/solution.py
+++ b/solution.py
@@ -9,7 +9,7 @@
 
 root_two_pi = math.sqrt(2.0 / math.pi)
 cubic = 0.044715
-chips = ("col", "x")
+chips = ("x", "col")
 bf16 = jnp.bfloat16
 f32 = jnp.float32
 mib = 1024 * 1024
@@ -54,13 +54,6 @@
         compiler_params=pltpu.CompilerParams(vmem_limit_bytes=limit * mib),
         name=name,
     )(*args)
-
-
-def spread_kernel(tokens_ref, cotangent_ref, out_ref):
-    both = jnp.concatenate([tokens_ref[...].astype(f32), cotangent_ref[...].astype(f32)], axis=0)
-    both = both.astype(bf16)
-    for chip in range(out_ref.shape[0]):
-        out_ref[chip] = both
 
 
 def terms_kernel(share, acts_ref, in_ref, out_ref, in_far_ref, out_far_ref, terms_ref):
@@ -128,13 +121,14 @@
     held = 2 * share * count
     shaped = lambda *dims: jax.ShapeDtypeStruct(dims, bf16)
 
-    copies = whole(
-        spread_kernel, "spread_rows", shaped(count, 2 * share, width), (tokens, cotangent), 0
-    )
+    both = jnp.concatenate([tokens, cotangent], axis=0)
     weight_in_far = other_core(weight_in)
     weight_out_far = other_core(weight_out)
     weights = (weight_in, weight_out, weight_in_far, weight_out_far)
-    acts = exchange(copies, chips).reshape(held, width)
+    cols, xs = lax.axis_size("col"), lax.axis_size("x")
+    line = exchange(jnp.broadcast_to(both[None], (cols,) + both.shape), "col")
+    line = line.reshape(1, held // xs, width)
+    acts = exchange(jnp.broadcast_to(line, (xs,) + line.shape[1:]), "x").reshape(held, width)
 
     partial = whole(
         bind(terms_kernel, share),

time: 109 us -> 104 us (0.954)
  the two profiles are of different devices: /device:TPU:2 before, /device:TPU:64 now
where the time goes in v4:
time: 104 us; the launch traced here: 103 us
  blocking collectives  66.7 us (64%)
  starting transfers between devices  15.2 us (15%)
  waiting for transfers between devices  11.4 us (11%)
  Pallas kernels  7.45 us (7%)
    all_to_all x4, blocking collectives, exchange(): return lax.all_to_all(blocks, axes, split_axis=0, concat_axis=0)  66.7 us
    all_to_all x1, waiting for transfers between devices, exchange(): return lax.all_to_all(blocks, axes, split_axis=0, concat_axis=0)  10.3 us
    ppermute x4, starting transfers between devices, other_core(): return lax.ppermute(block, 'core', [(0, 1), (1, 0)])  8.66 us
    pallas_call x4, Pallas kernels, whole(): pl.pallas_call(kernel, out_shape=out_shapes, in_specs=[in_vmem] * len(arg...  7.45 us
    all_to_all x1, starting transfers between devices, exchange(): return lax.all_to_all(blocks, axes, split_axis=0, concat_axis=0)  6.55 us
  transfers between devices with their start and end apart: 5, of which 2 were waited for; matrix products, arithmetic and copies ran while one was open for 1% of the time, Pallas kernels for 3%

profile of v4, /device:TPU:64, one launch (start us, length us, event | category | flops | bytes accessed | tf_op | source)
XLA Modules:
  0.0 103.1 jit_solution(3778507896077102076)
XLA Ops:
  0.6 1.9 %collective-permute-start = (bf16[1536,384]{1,0:T(8,128)(2,1)}, bf16[1536,384]{1,0:T(8,128)(2,1)S(1)}, u32[]{:S(2)}, u32[]{:S(2)}) collective-permute-start(bf16[1536,384]{1,0:T(8,128)(2,1)} %refs_1_.3), channel_id=1, source_target_pairs={{0,1},{1,0},{2,3},{3,2},{4,5},{5,4},{6,7},{7,6},{8,9},{9,8},{10,11... | collective-permute-start | bytes 3538952 | tf_op jit(solution)/shard_map/ppermute | solution.py:34
  2.6 2.4 %collective-permute-start.1 = (bf16[384,1536]{1,0:T(8,128)(2,1)}, bf16[384,1536]{1,0:T(8,128)(2,1)S(1)}, u32[]{:S(2)}, u32[]{:S(2)}) collective-permute-start(bf16[384,1536]{1,0:T(8,128)(2,1)} %refs_2_.3), channel_id=1, source_target_pairs={{0,1},{1,0},{2,3},{3,2},{4,5},{5,4},{6,7},{7,6},{8,9},{9,8},{10,11... | collective-permute-start | bytes 3538952 | tf_op jit(solution)/shard_map/ppermute | solution.py:34
  5.0 0.7 pad_maximum_fusion
  5.7 19.0 %all_to_all.25 = bf16[8,8,1536]{2,1,0:T(8,128)(2,1)S(1)} all-to-all(bf16[8,8,1536]{2,1,0:T(8,128)(2,1)S(1)} %broadcast_in_dim.6), channel_id=1, replica_groups=mesh['row'=8,'col'=8,'x'=4,'core'=2] {'col'}, dimensions={0} | all-to-all | bytes 393216 | tf_op jit(solution)/shard_map/all_to_all | solution.py:38
  24.7 0.0 copy-start
  24.7 0.0 copy-start.1
  24.7 0.1 broadcast_in_dim.15
  24.8 14.7 %all_to_all.26 = bf16[4,64,1536]{2,1,0:T(8,128)(2,1)S(1)} all-to-all(bf16[4,64,1536]{2,1,0:T(8,128)(2,1)S(1)} %broadcast_in_dim.15), channel_id=1, replica_groups=mesh['row'=8,'col'=8,'x'=4,'core'=2] {'x'}, dimensions={0} | all-to-all | bytes 1572864 | tf_op jit(solution)/shard_map/all_to_all | solution.py:38
  39.5 0.0 collective-permute-done.refs_3_
  39.5 0.0 collective-permute-done.1.refs_4_
  39.5 0.0 copy-done
  39.5 0.0 copy-done.1
  39.5 1.8 %hidden_terms.1 = bf16[256,768]{1,0:T(8,128)(2,1)S(1)} custom-call(bf16[256,1536]{1,0:T(8,128)(2,1)S(1)} %bitcast.7, bf16[1536,384]{1,0:T(8,128)(2,1)S(1)} %copy-done, bf16[384,1536]{1,0:T(8,128)(2,1)S(1)} %copy-done.1, bf16[1536,384]{1,0:T(8,128)(2,1)S(1)} %collective-permute-done.refs_3_, bf16[384,1536]{1,0:T(8,128)(2,1)S(1)} %collective-permute-done.1.refs_4_), custom_call_target="tpu_custom_call" | custom-call | flops 1207959552 | bytes 5898240 | tf_op jit(solution)/shard_map/hidden_terms/pallas_call | solution.py:48
  41.3 18.8 %all_to_all.27.refs_0_ = bf16[8,32,768]{2,1,0:T(8,128)(2,1)S(1)} all-to-all(bf16[8,32,768]{2,1,0:T(8,128)(2,1)S(1)} %bitcast.10), channel_id=1, replica_groups=mesh['row'=8,'col'=8,'x'=4,'core'=2] {'row'}, dimensions={0} | all-to-all | bytes 786432 | tf_op jit(solution)/shard_map/all_to_all | solution.py:38
  60.1 0.1 gelu_rows.1
  60.2 14.3 %all_to_all.28 = bf16[8,32,768]{2,1,0:T(8,128)(2,1)S(1)} all-to-all(bf16[8,32,768]{2,1,0:T(8,128)(2,1)S(1)} %gelu_rows.1), channel_id=1, replica_groups=mesh['row'=8,'col'=8,'x'=4,'core'=2] {'row'}, dimensions={0} | all-to-all | bytes 786432 | tf_op jit(solution)/shard_map/all_to_all | solution.py:38
  74.5 2.7 %output_terms.1 = bf16[256,1536]{1,0:T(8,128)(2,1)} custom-call(bf16[256,768]{1,0:T(8,128)(2,1)S(1)} %bitcast.5, bf16[1536,384]{1,0:T(8,128)(2,1)S(1)} %copy-done, bf16[384,1536]{1,0:T(8,128)(2,1)S(1)} %copy-done.1, bf16[1536,384]{1,0:T(8,128)(2,1)S(1)} %collective-permute-done.refs_3_, bf16[384,1536]{1,0:T(8,128)(2,1)S(1)} %collective-permute-done.1.refs_4_), custom_call_target="tpu_custom_call" | custom-call | flops 1207959552 | bytes 5898240 | tf_op jit(solution)/shard_map/output_terms/pallas_call | solution.py:48
  77.2 6.6 %all-to-all-start.4 = ((bf16[32,8,1536]{2,1,0:T(8,128)(2,1)}), bf16[32,8,1536]{2,1,0:T(8,128)(2,1)S(1)}, u32[]{:S(2)}, u32[]{:S(2)}) async-start(bf16[32,8,1536]{2,1,0:T(8,128)(2,1)} %bitcast.4), calls=%async_computation.4 | async-start | bytes 1572864 | tf_op jit(solution)/shard_map/all_to_all | solution.py:38
  83.7 1.9 %collective-permute-start.2 = (bf16[256,1536]{1,0:T(8,128)(2,1)S(1)}, bf16[256,1536]{1,0:T(8,128)(2,1)S(1)}, u32[]{:S(2)}, u32[]{:S(2)}) collective-permute-start(bf16[256,1536]{1,0:T(8,128)(2,1)S(1)} %bitcast.8), channel_id=1, source_target_pairs={{0,1},{1,0},{2,3},{3,2},{4,5},{5,4},{6,7},{7,6},{8,9},{9,8},{10,11... | collective-permute-start | bytes 2359304 | tf_op jit(solution)/shard_map/ppermute | solution.py:34
  85.7 2.4 %collective-permute-start.3 = (bf16[256,384]{1,0:T(8,128)(2,1)S(1)}, bf16[256,384]{1,0:T(8,128)(2,1)S(1)}, u32[]{:S(2)}, u32[]{:S(2)}) collective-permute-start(bf16[256,384]{1,0:T(8,128)(2,1)S(1)} %get-tuple-element.14), channel_id=1, source_target_pairs={{0,1},{1,0},{2,3},{3,2},{4,5},{5,4},{6,7},{7,6},{8,9},{9,8},{10,11... | collective-permute-start | bytes 589832 | tf_op jit(solution)/shard_map/ppermute | solution.py:34
  88.1 1.0 %collective-permute-done.3.refs_3_ = bf16[256,384]{1,0:T(8,128)(2,1)S(1)} collective-permute-done((bf16[256,384]{1,0:T(8,128)(2,1)S(1)}, bf16[256,384]{1,0:T(8,128)(2,1)S(1)}, u32[]{:S(2)}, u32[]{:S(2)}) %collective-permute-start.3) | collective-permute-done | bytes 196640 | tf_op jit(solution)/shard_map/ppermute | solution.py:34
  89.2 0.0 collective-permute-done.2.refs_1_
  89.2 2.8 %weight_gradients.1 = (bf16[1536,384]{1,0:T(8,128)(2,1)}, bf16[384,1536]{1,0:T(8,128)(2,1)}) custom-call(bf16[256,1536]{1,0:T(8,128)(2,1)S(1)} %bitcast.9, bf16[256,1536]{1,0:T(8,128)(2,1)S(1)} %collective-permute-done.2.refs_1_, bf16[256,384]{1,0:T(8,128)(2,1)S(1)} %get-tuple-element.15.refs_2_, bf16[256,384]{1,0:T(8,128)(2,1)S(1)} %collective-permute-done.3.refs_3_), custom_call_target="tpu_custom_call" | custom-call | flops 1207959552 | bytes 4325376 | tf_op jit(solution)/shard_map/weight_gradients/pallas_call | solution.py:48
  92.0 10.3 %all-to-all-done.4 = bf16[32,8,1536]{2,1,0:T(8,128)(2,1)S(1)} async-done(((bf16[32,8,1536]{2,1,0:T(8,128)(2,1)}), bf16[32,8,1536]{2,1,0:T(8,128)(2,1)S(1)}, u32[]{:S(2)}, u32[]{:S(2)}) %all-to-all-start.4) | async-done | bytes 786464 | tf_op jit(solution)/shard_map/all_to_all | solution.py:38
  102.4 0.1 reduce_sum.12
  102.5 0.6 fusion.1
  (2 shorter events, 0.1 us)
Async XLA Ops:
  0.6 38.9 %collective-permute-start = (bf16[1536,384]{1,0:T(8,128)(2,1)}, bf16[1536,384]{1,0:T(8,128)(2,1)S(1)}, u32[]{:S(2)}, u32[]{:S(2)}) collective-permute-start(bf16[1536,384]{1,0:T(8,128)(2,1)} %refs_1_.3), channel_id=1, source_target_pairs={{0,1},{1,0},{2,3},{3,2},{4,5},{5,4},{6,7},{7,6},{8,9},{9,8},{10,11... | collective-permute-start | bytes 3538952 | tf_op jit(solution)/shard_map/ppermute | solution.py:34
  2.6 36.9 %collective-permute-start.1 = (bf16[384,1536]{1,0:T(8,128)(2,1)}, bf16[384,1536]{1,0:T(8,128)(2,1)S(1)}, u32[]{:S(2)}, u32[]{:S(2)}) collective-permute-start(bf16[384,1536]{1,0:T(8,128)(2,1)} %refs_2_.3), channel_id=1, source_target_pairs={{0,1},{1,0},{2,3},{3,2},{4,5},{5,4},{6,7},{7,6},{8,9},{9,8},{10,11... | collective-permute-start | bytes 3538952 | tf_op jit(solution)/shard_map/ppermute | solution.py:34
  24.7 14.8 %copy-start = (bf16[1536,384]{1,0:T(8,128)(2,1)S(1)}, bf16[1536,384]{1,0:T(8,128)(2,1)}, u32[]{:S(2)}) copy-start(bf16[1536,384]{1,0:T(8,128)(2,1)} %refs_1_.3) | copy-start | bytes 3538948
  24.7 14.8 %copy-start.1 = (bf16[384,1536]{1,0:T(8,128)(2,1)S(1)}, bf16[384,1536]{1,0:T(8,128)(2,1)}, u32[]{:S(2)}) copy-start(bf16[384,1536]{1,0:T(8,128)(2,1)} %refs_2_.3) | copy-start | bytes 3538948
  77.2 25.2 %all-to-all-start.4 = ((bf16[32,8,1536]{2,1,0:T(8,128)(2,1)}), bf16[32,8,1536]{2,1,0:T(8,128)(2,1)S(1)}, u32[]{:S(2)}, u32[]{:S(2)}) async-start(bf16[32,8,1536]{2,1,0:T(8,128)(2,1)} %bitcast.4), calls=%async_computation.4 | async-start | bytes 1572864 | tf_op jit(solution)/shard_map/all_to_all | solution.py:38
  83.7 5.4 %collective-permute-start.2 = (bf16[256,1536]{1,0:T(8,128)(2,1)S(1)}, bf16[256,1536]{1,0:T(8,128)(2,1)S(1)}, u32[]{:S(2)}, u32[]{:S(2)}) collective-permute-start(bf16[256,1536]{1,0:T(8,128)(2,1)S(1)} %bitcast.8), channel_id=1, source_target_pairs={{0,1},{1,0},{2,3},{3,2},{4,5},{5,4},{6,7},{7,6},{8,9},{9,8},{10,11... | collective-permute-start | bytes 2359304 | tf_op jit(solution)/shard_map/ppermute | solution.py:34
  85.7 3.5 %collective-permute-start.3 = (bf16[256,384]{1,0:T(8,128)(2,1)S(1)}, bf16[256,384]{1,0:T(8,128)(2,1)S(1)}, u32[]{:S(2)}, u32[]{:S(2)}) collective-permute-start(bf16[256,384]{1,0:T(8,128)(2,1)S(1)} %get-tuple-element.14), channel_id=1, source_target_pairs={{0,1},{1,0},{2,3},{3,2},{4,5},{5,4},{6,7},{7,6},{8,9},{9,8},{10,11... | collective-permute-start | bytes 589832 | tf_op jit(solution)/shard_map/ppermute | solution.py:34

commit v5 on v4

--- a/solution.py
+++ b/solution.py
@@ -13,6 +13,7 @@
 bf16 = jnp.bfloat16
 f32 = jnp.float32
 mib = 1024 * 1024
+swap_cover = 24_000_000_000
 
 
 def gelu_parts(hidden):
@@ -42,18 +43,24 @@
     return lax.broadcasted_iota(jnp.int32, shape, 0) % (2 * share) < share
 
 
-def whole(kernel, name, out_shapes, args, products, limit=24):
+def whole(kernel, name, out_shapes, args, flops, out_specs=None, scratch=(), limit=24):
+    moved = sum(2 * math.prod(a.shape) for a in (*args, *jax.tree.leaves(out_shapes)))
     in_vmem = pl.BlockSpec(memory_space=pltpu.VMEM)
-    moved = sum(a.size * a.dtype.itemsize for a in (*args, *jax.tree.leaves(out_shapes)))
     return pl.pallas_call(
         kernel,
         out_shape=out_shapes,
         in_specs=[in_vmem] * len(args),
-        out_specs=jax.tree.map(lambda _: in_vmem, out_shapes),
-        cost_estimate=pl.CostEstimate(flops=2 * products, bytes_accessed=moved, transcendentals=0),
+        out_specs=out_specs or jax.tree.map(lambda _: in_vmem, out_shapes),
+        scratch_shapes=list(scratch),
+        cost_estimate=pl.CostEstimate(flops=flops, bytes_accessed=moved, transcendentals=0),
         compiler_params=pltpu.CompilerParams(vmem_limit_bytes=limit * mib),
         name=name,
     )(*args)
+
+
+def spread_kernel(block_ref, out_ref):
+    for place in range(out_ref.shape[0]):
+        out_ref[place] = block_ref[...]
 
 
 def terms_kernel(share, acts_ref, in_ref, out_ref, in_far_ref, out_far_ref, terms_ref):
@@ -78,16 +85,26 @@
         out_ref[row] = made
 
 
-def sums_kernel(share, made_ref, in_ref, out_ref, in_far_ref, out_far_ref, sums_ref):
+def sums_kernel(
+    share, made_ref, in_ref, out_ref, in_far_ref, out_far_ref, sums_hbm, sums_ref, sems
+):
     units, width = out_ref.shape
     near, far = made_ref[:, :units], made_ref[:, units:]
     step = 512
-    for start in range(0, width, step):
+    stores = []
+    for place, start in enumerate(range(0, width, step)):
         part = slice(start, start + step)
         ahead = contract(near, out_ref[:, part], 1, 0) + contract(far, out_far_ref[:, part], 1, 0)
         back = contract(near, in_ref[part, :], 1, 1) + contract(far, in_far_ref[part, :], 1, 1)
         picked = jnp.where(first_kind(ahead.shape, share), ahead, back)
         sums_ref[:, part] = picked.astype(bf16)
+        store = pltpu.make_async_copy(
+            sums_ref.at[:, part], sums_hbm.at[:, part], sems.at[place]
+        )
+        store.start()
+        stores.append(store)
+    for store in stores:
+        store.wait()
 
 
 def weight_kernel(share, acts_ref, acts_far_ref, made_ref, made_far_ref, grad_in_ref, grad_out_ref):
@@ -127,15 +144,16 @@
     weights = (weight_in, weight_out, weight_in_far, weight_out_far)
     cols, xs = lax.axis_size("col"), lax.axis_size("x")
     line = exchange(jnp.broadcast_to(both[None], (cols,) + both.shape), "col")
-    line = line.reshape(1, held // xs, width)
-    acts = exchange(jnp.broadcast_to(line, (xs,) + line.shape[1:]), "x").reshape(held, width)
+    line = line.reshape(held // xs, width)
+    line = whole(spread_kernel, "spread_rows", shaped(xs, *line.shape), (line,), swap_cover)
+    acts = exchange(line, "x").reshape(held, width)
 
     partial = whole(
         bind(terms_kernel, share),
         "hidden_terms",
         shaped(held, 2 * units),
         (acts, *weights),
-        4 * held * width * units,
+        8 * held * width * units,
     )
     received = exchange(partial.reshape(rows, held // rows, 2 * units), "row")
     made = whole(
@@ -146,9 +164,11 @@
     sums = whole(
         bind(sums_kernel, share),
         "output_terms",
-        shaped(held, width),
+        pltpu.HBM((held, width), bf16),
         (made, *weights),
-        4 * held * width * units,
+        8 * held * width * units,
+        out_specs=pl.BlockSpec(memory_space=pltpu.HBM),
+        scratch=(pltpu.VMEM((held, width), bf16), pltpu.SemaphoreType.DMA((width // 512,))),
     )
     sums, made, acts = lax.optimization_barrier((sums, made, acts))
     blocks = exchange(sums.reshape(count, 2 * share, width), chips)
@@ -161,7 +181,7 @@
         "weight_gradients",
         (shaped(width, units), shaped(units, width)),
         (acts, acts_far, made[:, :units], made_far),
-        4 * held * width * units,
+        8 * held * width * units,
     )
     return final[:share], final[share:], grad_weight_in, grad_weight_out
 

time: 104 us -> 99.7 us (0.959)
  blocking collectives: 66.7 us -> 47.4 us
  starting transfers between devices: 15.2 us -> 25.3 us
  waiting for transfers between devices: 11.4 us -> 16.1 us
    all_to_all x4 -> x3, blocking collectives: 66.7 us -> 47.4 us  [exchange(): return lax.all_to_all(blocks, axes, split_axis=0, concat_axis=0)]
    all_to_all x1 -> x2, starting transfers between devices: 6.55 us -> 16.6 us  [exchange(): return lax.all_to_all(blocks, axes, split_axis=0, concat_axis=0)]
    all_to_all x1 -> x2, waiting for transfers between devices: 10.3 us -> 15 us  [exchange(): return lax.all_to_all(blocks, axes, split_axis=0, concat_axis=0)]
    pallas_call x4 -> x5, Pallas kernels: 7.45 us -> 7.35 us  [whole(): pl.pallas_call(kernel, out_shape=out_shapes, in_specs=[in_vmem] * len(arg...]
  transfers between devices with their start and end apart: 5 -> 6, of which waited for: 2 -> 3; matrix products, arithmetic and copies ran while one was open for 1% -> 0% of each run, Pallas kernels for 3% -> 3%
where the time goes in v5:
time: 99.7 us; the launch traced here: 99.1 us
  blocking collectives  47.4 us (48%)
  starting transfers between devices  25.3 us (25%)
  waiting for transfers between devices  16.1 us (16%)
  Pallas kernels  7.35 us (7%)
  local copies, waits for them, and re-layouts  1.36 us (1%)
    all_to_all x3, blocking collectives, exchange(): return lax.all_to_all(blocks, axes, split_axis=0, concat_axis=0)  47.4 us
    all_to_all x2, starting transfers between devices, exchange(): return lax.all_to_all(blocks, axes, split_axis=0, concat_axis=0)  16.6 us
    all_to_all x2, waiting for transfers between devices, exchange(): return lax.all_to_all(blocks, axes, split_axis=0, concat_axis=0)  15 us
    ppermute x4, starting transfers between devices, other_core(): return lax.ppermute(block, 'core', [(0, 1), (1, 0)])  8.65 us
    pallas_call x5, Pallas kernels, whole(): pl.pallas_call(kernel, out_shape=out_shapes, in_specs=[in_vmem] * len(arg...  7.35 us
  transfers between devices with their start and end apart: 6, of which 3 were waited for; matrix products, arithmetic and copies ran while one was open for 0% of the time, Pallas kernels for 3%

profile of v5, /device:TPU:64, one launch (start us, length us, event | category | flops | bytes accessed | tf_op | source)
XLA Modules:
  0.0 99.1 jit_solution(245971956123654997)
XLA Ops:
  0.6 0.7 pad_maximum_fusion
  1.4 0.7 broadcast_in_dim.2
  2.1 10.0 %all-to-all-start = ((bf16[8,8,1536]{2,1,0:T(8,128)(2,1)}), bf16[8,8,1536]{2,1,0:T(8,128)(2,1)S(1)}, u32[]{:S(2)}, u32[]{:S(2)}) async-start(bf16[8,8,1536]{2,1,0:T(8,128)(2,1)} %broadcast_in_dim.2), calls=%async_computation | async-start | bytes 393216 | tf_op jit(solution)/shard_map/all_to_all | solution.py:39
  12.0 1.9 %collective-permute-start = (bf16[1536,384]{1,0:T(8,128)(2,1)}, bf16[1536,384]{1,0:T(8,128)(2,1)S(1)}, u32[]{:S(2)}, u32[]{:S(2)}) collective-permute-start(bf16[1536,384]{1,0:T(8,128)(2,1)} %refs_1_.3), channel_id=1, source_target_pairs={{0,1},{1,0},{2,3},{3,2},{4,5},{5,4},{6,7},{7,6},{8,9},{9,8},{10,11... | collective-permute-start | bytes 3538952 | tf_op jit(solution)/shard_map/ppermute | solution.py:35
  13.9 2.4 %collective-permute-start.1 = (bf16[384,1536]{1,0:T(8,128)(2,1)}, bf16[384,1536]{1,0:T(8,128)(2,1)S(1)}, u32[]{:S(2)}, u32[]{:S(2)}) collective-permute-start(bf16[384,1536]{1,0:T(8,128)(2,1)} %refs_2_.3), channel_id=1, source_target_pairs={{0,1},{1,0},{2,3},{3,2},{4,5},{5,4},{6,7},{7,6},{8,9},{9,8},{10,11... | collective-permute-start | bytes 3538952 | tf_op jit(solution)/shard_map/ppermute | solution.py:35
  16.4 4.7 %all-to-all-done = bf16[8,8,1536]{2,1,0:T(8,128)(2,1)S(1)} async-done(((bf16[8,8,1536]{2,1,0:T(8,128)(2,1)}), bf16[8,8,1536]{2,1,0:T(8,128)(2,1)S(1)}, u32[]{:S(2)}, u32[]{:S(2)}) %all-to-all-start) | async-done | bytes 196640 | tf_op jit(solution)/shard_map/all_to_all | solution.py:39
  21.0 0.0 copy-start.1
  21.1 0.1 spread_rows.1
  21.1 0.0 copy-start
  21.1 14.4 %all_to_all.25 = bf16[4,64,1536]{2,1,0:T(8,128)(2,1)S(1)} all-to-all(bf16[4,64,1536]{2,1,0:T(8,128)(2,1)S(1)} %spread_rows.1), channel_id=1, replica_groups=mesh['row'=8,'col'=8,'x'=4,'core'=2] {'x'}, dimensions={0} | all-to-all | bytes 1572864 | tf_op jit(solution)/shard_map/all_to_all | solution.py:39
  35.5 0.0 collective-permute-done.refs_3_
  35.5 0.0 collective-permute-done.1.refs_4_
  35.5 0.0 copy-done.1
  35.5 0.0 copy-done
  35.5 1.8 %hidden_terms.1 = bf16[256,768]{1,0:T(8,128)(2,1)S(1)} custom-call(bf16[256,1536]{1,0:T(8,128)(2,1)S(1)} %bitcast.7, bf16[1536,384]{1,0:T(8,128)(2,1)S(1)} %copy-done, bf16[384,1536]{1,0:T(8,128)(2,1)S(1)} %copy-done.1, bf16[1536,384]{1,0:T(8,128)(2,1)S(1)} %collective-permute-done.refs_3_, bf16[384,1536]{1,0:T(8,128)(2,1)S(1)} %collective-permute-done.1.refs_4_), custom_call_target="tpu_custom_call" | custom-call | flops 1207959552 | bytes 5898240 | tf_op jit(solution)/shard_map/hidden_terms/pallas_call | solution.py:49
  37.3 18.8 %all_to_all.26.refs_0_ = bf16[8,32,768]{2,1,0:T(8,128)(2,1)S(1)} all-to-all(bf16[8,32,768]{2,1,0:T(8,128)(2,1)S(1)} %bitcast.10), channel_id=1, replica_groups=mesh['row'=8,'col'=8,'x'=4,'core'=2] {'row'}, dimensions={0} | all-to-all | bytes 786432 | tf_op jit(solution)/shard_map/all_to_all | solution.py:39
  56.1 0.1 gelu_rows.1
  56.3 14.3 %all_to_all.27 = bf16[8,32,768]{2,1,0:T(8,128)(2,1)S(1)} all-to-all(bf16[8,32,768]{2,1,0:T(8,128)(2,1)S(1)} %gelu_rows.1), channel_id=1, replica_groups=mesh['row'=8,'col'=8,'x'=4,'core'=2] {'row'}, dimensions={0} | all-to-all | bytes 786432 | tf_op jit(solution)/shard_map/all_to_all | solution.py:39
  70.5 2.5 %output_terms.1 = bf16[256,1536]{1,0:T(8,128)(2,1)} custom-call(bf16[256,768]{1,0:T(8,128)(2,1)S(1)} %bitcast.5, bf16[1536,384]{1,0:T(8,128)(2,1)S(1)} %copy-done, bf16[384,1536]{1,0:T(8,128)(2,1)S(1)} %copy-done.1, bf16[1536,384]{1,0:T(8,128)(2,1)S(1)} %collective-permute-done.refs_3_, bf16[384,1536]{1,0:T(8,128)(2,1)S(1)} %collective-permute-done.1.refs_4_), custom_call_target="tpu_custom_call" | custom-call | flops 1207959552 | bytes 5898240 | tf_op jit(solution)/shard_map/output_terms/pallas_call | solution.py:49
  73.1 6.7 %all-to-all-start.4 = ((bf16[32,8,1536]{2,1,0:T(8,128)(2,1)}), bf16[32,8,1536]{2,1,0:T(8,128)(2,1)S(1)}, u32[]{:S(2)}, u32[]{:S(2)}) async-start(bf16[32,8,1536]{2,1,0:T(8,128)(2,1)} %bitcast.12), calls=%async_computation.4 | async-start | bytes 1572864 | tf_op jit(solution)/shard_map/all_to_all | solution.py:39
  79.7 1.9 %collective-permute-start.2 = (bf16[256,1536]{1,0:T(8,128)(2,1)S(1)}, bf16[256,1536]{1,0:T(8,128)(2,1)S(1)}, u32[]{:S(2)}, u32[]{:S(2)}) collective-permute-start(bf16[256,1536]{1,0:T(8,128)(2,1)S(1)} %bitcast.8), channel_id=1, source_target_pairs={{0,1},{1,0},{2,3},{3,2},{4,5},{5,4},{6,7},{7,6},{8,9},{9,8},{10,11... | collective-permute-start | bytes 2359304 | tf_op jit(solution)/shard_map/ppermute | solution.py:35
  81.7 2.4 %collective-permute-start.3 = (bf16[256,384]{1,0:T(8,128)(2,1)S(1)}, bf16[256,384]{1,0:T(8,128)(2,1)S(1)}, u32[]{:S(2)}, u32[]{:S(2)}) collective-permute-start(bf16[256,384]{1,0:T(8,128)(2,1)S(1)} %get-tuple-element.14), channel_id=1, source_target_pairs={{0,1},{1,0},{2,3},{3,2},{4,5},{5,4},{6,7},{7,6},{8,9},{9,8},{10,11... | collective-permute-start | bytes 589832 | tf_op jit(solution)/shard_map/ppermute | solution.py:35
  84.1 1.0 %collective-permute-done.3.refs_3_ = bf16[256,384]{1,0:T(8,128)(2,1)S(1)} collective-permute-done((bf16[256,384]{1,0:T(8,128)(2,1)S(1)}, bf16[256,384]{1,0:T(8,128)(2,1)S(1)}, u32[]{:S(2)}, u32[]{:S(2)}) %collective-permute-start.3) | collective-permute-done | bytes 196640 | tf_op jit(solution)/shard_map/ppermute | solution.py:35
  85.2 0.0 collective-permute-done.2.refs_1_
  85.2 2.8 %weight_gradients.1 = (bf16[1536,384]{1,0:T(8,128)(2,1)}, bf16[384,1536]{1,0:T(8,128)(2,1)}) custom-call(bf16[256,1536]{1,0:T(8,128)(2,1)S(1)} %bitcast.9, bf16[256,1536]{1,0:T(8,128)(2,1)S(1)} %collective-permute-done.2.refs_1_, bf16[256,384]{1,0:T(8,128)(2,1)S(1)} %get-tuple-element.15.refs_2_, bf16[256,384]{1,0:T(8,128)(2,1)S(1)} %collective-permute-done.3.refs_3_), custom_call_target="tpu_custom_call" | custom-call | flops 1207959552 | bytes 4325376 | tf_op jit(solution)/shard_map/weight_gradients/pallas_call | solution.py:49
  88.0 10.3 %all-to-all-done.4 = bf16[32,8,1536]{2,1,0:T(8,128)(2,1)S(1)} async-done(((bf16[32,8,1536]{2,1,0:T(8,128)(2,1)}), bf16[32,8,1536]{2,1,0:T(8,128)(2,1)S(1)}, u32[]{:S(2)}, u32[]{:S(2)}) %all-to-all-start.4) | async-done | bytes 786464 | tf_op jit(solution)/shard_map/all_to_all | solution.py:39
  98.4 0.1 reduce_sum.12
  98.5 0.6 fusion.1
  (1 shorter events, 0.0 us)
Async XLA Ops:
  2.1 19.0 %all-to-all-start = ((bf16[8,8,1536]{2,1,0:T(8,128)(2,1)}), bf16[8,8,1536]{2,1,0:T(8,128)(2,1)S(1)}, u32[]{:S(2)}, u32[]{:S(2)}) async-start(bf16[8,8,1536]{2,1,0:T(8,128)(2,1)} %broadcast_in_dim.2), calls=%async_computation | async-start | bytes 393216 | tf_op jit(solution)/shard_map/all_to_all | solution.py:39
  12.0 23.5 %collective-permute-start = (bf16[1536,384]{1,0:T(8,128)(2,1)}, bf16[1536,384]{1,0:T(8,128)(2,1)S(1)}, u32[]{:S(2)}, u32[]{:S(2)}) collective-permute-start(bf16[1536,384]{1,0:T(8,128)(2,1)} %refs_1_.3), channel_id=1, source_target_pairs={{0,1},{1,0},{2,3},{3,2},{4,5},{5,4},{6,7},{7,6},{8,9},{9,8},{10,11... | collective-permute-start | bytes 3538952 | tf_op jit(solution)/shard_map/ppermute | solution.py:35
  13.9 21.6 %collective-permute-start.1 = (bf16[384,1536]{1,0:T(8,128)(2,1)}, bf16[384,1536]{1,0:T(8,128)(2,1)S(1)}, u32[]{:S(2)}, u32[]{:S(2)}) collective-permute-start(bf16[384,1536]{1,0:T(8,128)(2,1)} %refs_2_.3), channel_id=1, source_target_pairs={{0,1},{1,0},{2,3},{3,2},{4,5},{5,4},{6,7},{7,6},{8,9},{9,8},{10,11... | collective-permute-start | bytes 3538952 | tf_op jit(solution)/shard_map/ppermute | solution.py:35
  21.0 14.5 %copy-start.1 = (bf16[384,1536]{1,0:T(8,128)(2,1)S(1)}, bf16[384,1536]{1,0:T(8,128)(2,1)}, u32[]{:S(2)}) copy-start(bf16[384,1536]{1,0:T(8,128)(2,1)} %refs_2_.3) | copy-start | bytes 3538948
  21.1 14.4 %copy-start = (bf16[1536,384]{1,0:T(8,128)(2,1)S(1)}, bf16[1536,384]{1,0:T(8,128)(2,1)}, u32[]{:S(2)}) copy-start(bf16[1536,384]{1,0:T(8,128)(2,1)} %refs_1_.3) | copy-start | bytes 3538948
  73.1 25.3 %all-to-all-start.4 = ((bf16[32,8,1536]{2,1,0:T(8,128)(2,1)}), bf16[32,8,1536]{2,1,0:T(8,128)(2,1)S(1)}, u32[]{:S(2)}, u32[]{:S(2)}) async-start(bf16[32,8,1536]{2,1,0:T(8,128)(2,1)} %bitcast.12), calls=%async_computation.4 | async-start | bytes 1572864 | tf_op jit(solution)/shard_map/all_to_all | solution.py:39
  79.7 5.4 %collective-permute-start.2 = (bf16[256,1536]{1,0:T(8,128)(2,1)S(1)}, bf16[256,1536]{1,0:T(8,128)(2,1)S(1)}, u32[]{:S(2)}, u32[]{:S(2)}) collective-permute-start(bf16[256,1536]{1,0:T(8,128)(2,1)S(1)} %bitcast.8), channel_id=1, source_target_pairs={{0,1},{1,0},{2,3},{3,2},{4,5},{5,4},{6,7},{7,6},{8,9},{9,8},{10,11... | collective-permute-start | bytes 2359304 | tf_op jit(solution)/shard_map/ppermute | solution.py:35
  81.7 3.5 %collective-permute-start.3 = (bf16[256,384]{1,0:T(8,128)(2,1)S(1)}, bf16[256,384]{1,0:T(8,128)(2,1)S(1)}, u32[]{:S(2)}, u32[]{:S(2)}) collective-permute-start(bf16[256,384]{1,0:T(8,128)(2,1)S(1)} %get-tuple-element.14), channel_id=1, source_target_pairs={{0,1},{1,0},{2,3},{3,2},{4,5},{5,4},{6,7},{7,6},{8,9},{9,8},{10,11... | collective-permute-start | bytes 589832 | tf_op jit(solution)/shard_map/ppermute | solution.py:35

commit v6 on v5

v6 whole, which is shorter than its diff:
```python
import math

import jax
import jax.numpy as jnp
from jax import lax
from jax.experimental import pallas as pl
from jax.experimental.pallas import tpu as pltpu
from jax.sharding import Mesh, PartitionSpec as P

root_two_pi = math.sqrt(2.0 / math.pi)
cubic = 0.044715
chips = ("x", "col")
bf16 = jnp.bfloat16
f32 = jnp.float32
mib = 1024 * 1024
swap_cover = 24_000_000_000


def gelu_parts(hidden):
    inner = jnp.tanh(root_two_pi * (hidden + cubic * hidden * hidden * hidden))
    value = 0.5 * hidden * (1.0 + inner)
    slope = 0.5 * (1.0 + inner) + 0.5 * hidden * (1.0 - inner * inner) * root_two_pi * (
        1.0 + 3.0 * cubic * hidden * hidden
    )
    return value, slope


def contract(left, right, left_dim, right_dim):
    return lax.dot_general(
        left, right, (((left_dim,), (right_dim,)), ((), ())), preferred_element_type=f32
    )


def other_core(block):
    return lax.ppermute(block, "core", [(0, 1), (1, 0)])


def exchange(blocks, axes):
    return lax.all_to_all(blocks, axes, split_axis=0, concat_axis=0)


def whole(kernel, name, out_shapes, args, flops, out_specs=None, scratch=(), limit=24):
    moved = sum(2 * math.prod(a.shape) for a in (*args, *jax.tree.leaves(out_shapes)))
    in_vmem = pl.BlockSpec(memory_space=pltpu.VMEM)
    return pl.pallas_call(
        kernel,
        out_shape=out_shapes,
        in_specs=[in_vmem] * len(args),
        out_specs=out_specs or jax.tree.map(lambda _: in_vmem, out_shapes),
        scratch_shapes=list(scratch),
        cost_estimate=pl.CostEstimate(flops=flops, bytes_accessed=moved, transcendentals=0),
        compiler_params=pltpu.CompilerParams(vmem_limit_bytes=limit * mib),
        name=name,
    )(*args)


def pairs_of(rows, group):
    pairs = rows.reshape(rows.shape[0] // (2 * group), 2, group, rows.shape[1])
    return pairs[:, 0], pairs[:, 1]


def meet(upper, lower, group):
    first = lax.broadcasted_iota(jnp.int32, upper.shape, 1) < group // 2
    return jnp.where(first, upper, lower)


def turned(groups):
    return pltpu.roll(groups, groups.shape[1] // 2, 1)


def kinds_of(ref, blocks, columns=slice(None)):
    size = ref.shape[0] // blocks
    return [
        jnp.concatenate(
            [
                ref[block * size + kind * size // 2 : block * size + (kind + 1) * size // 2, columns]
                for block in range(blocks)
            ],
            axis=0,
        )
        for kind in range(2)
    ]


def spread_kernel(share, line_ref, out_ref):
    group = 2 * share
    even, odd = pairs_of(line_ref[...].astype(f32), group)
    half = out_ref.shape[1] // 2
    tokens = meet(even, turned(odd), group).reshape(half, -1).astype(bf16)
    cotangent = meet(turned(even), odd, group).reshape(half, -1).astype(bf16)
    for place in range(out_ref.shape[0]):
        out_ref[place, :half] = tokens
        out_ref[place, half:] = cotangent


def terms_kernel(lines, rows, acts_ref, in_ref, out_ref, in_far_ref, out_far_ref, terms_ref):
    tokens, cotangent = kinds_of(acts_ref, lines)
    units = in_ref.shape[1]
    size = terms_ref.shape[0] // rows
    half = size // 2
    for place, (w_in, w_out) in enumerate(((in_ref, out_ref), (in_far_ref, out_far_ref))):
        columns = slice(place * units, (place + 1) * units)
        made = (contract(tokens, w_in[...], 1, 0), contract(cotangent, w_out[...], 1, 1))
        for kind, term in enumerate(made):
            term = term.astype(bf16)
            for row in range(rows):
                start = row * size + kind * half
                terms_ref[start : start + half, columns] = term[row * half : (row + 1) * half]


def gelu_kernel(terms_ref, out_ref):
    total = terms_ref[0].astype(f32)
    for row in range(1, terms_ref.shape[0]):
        total = total + terms_ref[row].astype(f32)
    half = total.shape[0] // 2
    value, slope = gelu_parts(total[:half])
    made = jnp.concatenate([value, total[half:] * slope], axis=0).astype(bf16)
    for row in range(out_ref.shape[0]):
        out_ref[row] = made


def sums_kernel(
    share, rows, made_ref, in_ref, out_ref, in_far_ref, out_far_ref, sums_hbm, sums_ref, sems
):
    units, width = out_ref.shape
    active, grads = kinds_of(made_ref, rows)
    group = 2 * share
    step = 512
    stores = []
    for place, start in enumerate(range(0, width, step)):
        part = slice(start, start + step)
        ahead = contract(active[:, :units], out_ref[:, part], 1, 0)
        ahead = ahead + contract(active[:, units:], out_far_ref[:, part], 1, 0)
        back = contract(grads[:, :units], in_ref[part, :], 1, 1)
        back = back + contract(grads[:, units:], in_far_ref[part, :], 1, 1)
        ahead, back = (sums.reshape(-1, group, step) for sums in (ahead, back))
        even, odd = meet(ahead, turned(back), group), meet(turned(ahead), back, group)
        picked = jnp.stack([even, odd], axis=1).reshape(-1, step)
        sums_ref[:, part] = picked.astype(bf16)
        store = pltpu.make_async_copy(
            sums_ref.at[:, part], sums_hbm.at[:, part], sems.at[place]
        )
        store.start()
        stores.append(store)
    for store in stores:
        store.wait()


def weight_kernel(
    lines, rows, acts_ref, acts_far_ref, made_ref, made_far_ref, grad_in_ref, grad_out_ref
):
    made = zip(kinds_of(made_ref, rows), kinds_of(made_far_ref, rows))
    active, grads = (jnp.concatenate(sides, axis=0) for sides in made)
    active = active.astype(f32).T.astype(bf16)
    step = 512
    for start in range(0, acts_ref.shape[1], step):
        part = slice(start, start + step)
        acts = zip(kinds_of(acts_ref, lines, part), kinds_of(acts_far_ref, lines, part))
        tokens, cotangent = (jnp.concatenate(sides, axis=0) for sides in acts)
        grad_in_ref[part, :] = contract(tokens, grads, 0, 0).astype(bf16)
        grad_out_ref[:, part] = contract(active, cotangent, 1, 0).astype(bf16)


def bind(kernel, *sizes):
    return lambda *refs: kernel(*sizes, *refs)


def local(tokens, weight_in, weight_out, cotangent):
    rows = lax.axis_size("row")
    count = lax.axis_size("col") * lax.axis_size("x")
    share, width = tokens.shape
    units = weight_in.shape[1]
    held = 2 * share * count
    shaped = lambda *dims: jax.ShapeDtypeStruct(dims, bf16)

    both = jnp.concatenate([tokens, cotangent], axis=0)
    weight_in_far = other_core(weight_in)
    weight_out_far = other_core(weight_out)
    weights = (weight_in, weight_out, weight_in_far, weight_out_far)
    cols, xs = lax.axis_size("col"), lax.axis_size("x")
    line = exchange(jnp.broadcast_to(both[None], (cols,) + both.shape), "col")
    line = line.reshape(held // xs, width)
    line = whole(
        bind(spread_kernel, share), "spread_rows", shaped(xs, *line.shape), (line,), swap_cover
    )
    acts = exchange(line, "x").reshape(held, width)

    partial = whole(
        bind(terms_kernel, xs, rows),
        "hidden_terms",
        shaped(held, 2 * units),
        (acts, *weights),
        4 * held * width * units,
    )
    received = exchange(partial.reshape(rows, held // rows, 2 * units), "row")
    made = whole(
        gelu_kernel, "gelu_rows", shaped(*received.shape), (received,), 0
    )
    made = exchange(made, "row").reshape(held, 2 * units)

    sums = whole(
        bind(sums_kernel, share, rows),
        "output_terms",
        pltpu.HBM((held, width), bf16),
        (made, *weights),
        4 * held * width * units,
        out_specs=pl.BlockSpec(memory_space=pltpu.HBM),
        scratch=(pltpu.VMEM((held, width), bf16), pltpu.SemaphoreType.DMA((width // 512,))),
    )
    sums, made, acts = lax.optimization_barrier((sums, made, acts))
    blocks = exchange(sums.reshape(count, 2 * share, width), chips)
    final = jnp.sum(blocks.astype(f32), axis=0).astype(bf16)

    made_far = other_core(made[:, units:])
    acts_far = other_core(acts)
    grad_weight_in, grad_weight_out = whole(
        bind(weight_kernel, xs, rows),
        "weight_gradients",
        (shaped(width, units), shaped(units, width)),
        (acts, acts_far, made[:, :units], made_far),
        4 * held * width * units,
    )
    return final[:share], final[share:], grad_weight_in, grad_weight_out


def solution(mesh):
    sizes = dict(mesh.shape)
    finer = Mesh(
        mesh.devices.reshape(sizes["row"], sizes["col"], sizes["depth"] // 2, 2),
        ("row", "col", "x", "core"),
    )
    wide = ("col", "x", "core")
    placed = (P(wide, "row"), P("row", wide), P(wide, "row"), P(wide, "row"))
    return jax.shard_map(
        local,
        mesh=finer,
        in_specs=placed,
        out_specs=(P(wide, "row"), P(wide, "row"), P("row", wide), P(wide, "row")),
        check_vma=False,
    )
```

time: 99.7 us -> 98.6 us (0.989)
  Pallas kernels: 7.35 us -> 5.64 us
    pallas_call x5, Pallas kernels: 7.35 us -> 5.64 us  [whole(): pl.pallas_call(kernel, out_shape=out_shapes, in_specs=[in_vmem] * len(arg...]
  transfers between devices with their start and end apart: 6 -> 6, of which waited for: 3 -> 3; matrix products, arithmetic and copies ran while one was open for 0% -> 0% of each run, Pallas kernels for 3% -> 2%
where the time goes in v6:
time: 98.6 us; the launch traced here: 98 us
  blocking collectives  47.4 us (48%)
  starting transfers between devices  25.3 us (26%)
  waiting for transfers between devices  16.7 us (17%)
  Pallas kernels  5.64 us (6%)
  local copies, waits for them, and re-layouts  1.36 us (1%)
    all_to_all x3, blocking collectives, exchange(): return lax.all_to_all(blocks, axes, split_axis=0, concat_axis=0)  47.4 us
    all_to_all x2, starting transfers between devices, exchange(): return lax.all_to_all(blocks, axes, split_axis=0, concat_axis=0)  16.6 us
    all_to_all x2, waiting for transfers between devices, exchange(): return lax.all_to_all(blocks, axes, split_axis=0, concat_axis=0)  15.7 us
    ppermute x4, starting transfers between devices, other_core(): return lax.ppermute(block, 'core', [(0, 1), (1, 0)])  8.65 us
    pallas_call x5, Pallas kernels, whole(): pl.pallas_call(kernel, out_shape=out_shapes, in_specs=[in_vmem] * len(arg...  5.64 us
  transfers between devices with their start and end apart: 6, of which 3 were waited for; matrix products, arithmetic and copies ran while one was open for 0% of the time, Pallas kernels for 2%

profile of v6, /device:TPU:64, one launch (start us, length us, event | category | flops | bytes accessed | tf_op | source)
XLA Modules:
  0.0 98.0 jit_solution(11437761853681564878)
XLA Ops:
  0.6 0.7 pad_maximum_fusion
  1.4 0.7 broadcast_in_dim.2
  2.1 10.0 %all-to-all-start = ((bf16[8,8,1536]{2,1,0:T(8,128)(2,1)}), bf16[8,8,1536]{2,1,0:T(8,128)(2,1)S(1)}, u32[]{:S(2)}, u32[]{:S(2)}) async-start(bf16[8,8,1536]{2,1,0:T(8,128)(2,1)} %broadcast_in_dim.2), calls=%async_computation | async-start | bytes 393216 | tf_op jit(solution)/shard_map/all_to_all | solution.py:39
  12.0 1.9 %collective-permute-start = (bf16[1536,384]{1,0:T(8,128)(2,1)}, bf16[1536,384]{1,0:T(8,128)(2,1)S(1)}, u32[]{:S(2)}, u32[]{:S(2)}) collective-permute-start(bf16[1536,384]{1,0:T(8,128)(2,1)} %refs_1_.3), channel_id=1, source_target_pairs={{0,1},{1,0},{2,3},{3,2},{4,5},{5,4},{6,7},{7,6},{8,9},{9,8},{10,11... | collective-permute-start | bytes 3538952 | tf_op jit(solution)/shard_map/ppermute | solution.py:35
  13.9 2.4 %collective-permute-start.1 = (bf16[384,1536]{1,0:T(8,128)(2,1)}, bf16[384,1536]{1,0:T(8,128)(2,1)S(1)}, u32[]{:S(2)}, u32[]{:S(2)}) collective-permute-start(bf16[384,1536]{1,0:T(8,128)(2,1)} %refs_2_.3), channel_id=1, source_target_pairs={{0,1},{1,0},{2,3},{3,2},{4,5},{5,4},{6,7},{7,6},{8,9},{9,8},{10,11... | collective-permute-start | bytes 3538952 | tf_op jit(solution)/shard_map/ppermute | solution.py:35
  16.4 4.7 %all-to-all-done = bf16[8,8,1536]{2,1,0:T(8,128)(2,1)S(1)} async-done(((bf16[8,8,1536]{2,1,0:T(8,128)(2,1)}), bf16[8,8,1536]{2,1,0:T(8,128)(2,1)S(1)}, u32[]{:S(2)}, u32[]{:S(2)}) %all-to-all-start) | async-done | bytes 196640 | tf_op jit(solution)/shard_map/all_to_all | solution.py:39
  21.0 0.0 copy-start.1
  21.1 0.1 spread_rows.1
  21.1 0.0 copy-start
  21.1 14.4 %all_to_all.25 = bf16[4,64,1536]{2,1,0:T(8,128)(2,1)S(1)} all-to-all(bf16[4,64,1536]{2,1,0:T(8,128)(2,1)S(1)} %spread_rows.1), channel_id=1, replica_groups=mesh['row'=8,'col'=8,'x'=4,'core'=2] {'x'}, dimensions={0} | all-to-all | bytes 1572864 | tf_op jit(solution)/shard_map/all_to_all | solution.py:39
  35.5 0.0 collective-permute-done.refs_3_
  35.5 0.0 collective-permute-done.1.refs_4_
  35.5 0.0 copy-done.1
  35.5 0.0 copy-done
  35.5 1.2 %hidden_terms.1 = bf16[256,768]{1,0:T(8,128)(2,1)S(1)} custom-call(bf16[256,1536]{1,0:T(8,128)(2,1)S(1)} %bitcast.7, bf16[1536,384]{1,0:T(8,128)(2,1)S(1)} %copy-done, bf16[384,1536]{1,0:T(8,128)(2,1)S(1)} %copy-done.1, bf16[1536,384]{1,0:T(8,128)(2,1)S(1)} %collective-permute-done.refs_3_, bf16[384,1536]{1,0:T(8,128)(2,1)S(1)} %collective-permute-done.1.refs_4_), custom_call_target="tpu_custom_call" | custom-call | flops 603979776 | bytes 5898240 | tf_op jit(solution)/shard_map/hidden_terms/pallas_call | solution.py:45
  36.8 18.8 %all_to_all.26.terms_ref = bf16[8,32,768]{2,1,0:T(8,128)(2,1)S(1)} all-to-all(bf16[8,32,768]{2,1,0:T(8,128)(2,1)S(1)} %bitcast.10), channel_id=1, replica_groups=mesh['row'=8,'col'=8,'x'=4,'core'=2] {'row'}, dimensions={0} | all-to-all | bytes 786432 | tf_op jit(solution)/shard_map/all_to_all | solution.py:39
  55.5 0.1 gelu_rows.1
  55.6 14.3 %all_to_all.27 = bf16[8,32,768]{2,1,0:T(8,128)(2,1)S(1)} all-to-all(bf16[8,32,768]{2,1,0:T(8,128)(2,1)S(1)} %gelu_rows.1), channel_id=1, replica_groups=mesh['row'=8,'col'=8,'x'=4,'core'=2] {'row'}, dimensions={0} | all-to-all | bytes 786432 | tf_op jit(solution)/shard_map/all_to_all | solution.py:39
  69.9 2.1 %output_terms.1 = bf16[256,1536]{1,0:T(8,128)(2,1)} custom-call(bf16[256,768]{1,0:T(8,128)(2,1)S(1)} %bitcast.5, bf16[1536,384]{1,0:T(8,128)(2,1)S(1)} %copy-done, bf16[384,1536]{1,0:T(8,128)(2,1)S(1)} %copy-done.1, bf16[1536,384]{1,0:T(8,128)(2,1)S(1)} %collective-permute-done.refs_3_, bf16[384,1536]{1,0:T(8,128)(2,1)S(1)} %collective-permute-done.1.refs_4_), custom_call_target="tpu_custom_call" | custom-call | flops 603979776 | bytes 5898240 | tf_op jit(solution)/shard_map/output_terms/pallas_call | solution.py:45
  72.0 6.7 %all-to-all-start.4 = ((bf16[32,8,1536]{2,1,0:T(8,128)(2,1)}), bf16[32,8,1536]{2,1,0:T(8,128)(2,1)S(1)}, u32[]{:S(2)}, u32[]{:S(2)}) async-start(bf16[32,8,1536]{2,1,0:T(8,128)(2,1)} %bitcast.12), calls=%async_computation.4 | async-start | bytes 1572864 | tf_op jit(solution)/shard_map/all_to_all | solution.py:39
  78.7 1.9 %collective-permute-start.2 = (bf16[256,1536]{1,0:T(8,128)(2,1)S(1)}, bf16[256,1536]{1,0:T(8,128)(2,1)S(1)}, u32[]{:S(2)}, u32[]{:S(2)}) collective-permute-start(bf16[256,1536]{1,0:T(8,128)(2,1)S(1)} %bitcast.8), channel_id=1, source_target_pairs={{0,1},{1,0},{2,3},{3,2},{4,5},{5,4},{6,7},{7,6},{8,9},{9,8},{10,11... | collective-permute-start | bytes 2359304 | tf_op jit(solution)/shard_map/ppermute | solution.py:35
  80.6 2.4 %collective-permute-start.3 = (bf16[256,384]{1,0:T(8,128)(2,1)S(1)}, bf16[256,384]{1,0:T(8,128)(2,1)S(1)}, u32[]{:S(2)}, u32[]{:S(2)}) collective-permute-start(bf16[256,384]{1,0:T(8,128)(2,1)S(1)} %get-tuple-element.14), channel_id=1, source_target_pairs={{0,1},{1,0},{2,3},{3,2},{4,5},{5,4},{6,7},{7,6},{8,9},{9,8},{10,11... | collective-permute-start | bytes 589832 | tf_op jit(solution)/shard_map/ppermute | solution.py:35
  83.0 1.0 %collective-permute-done.3.refs_3_ = bf16[256,384]{1,0:T(8,128)(2,1)S(1)} collective-permute-done((bf16[256,384]{1,0:T(8,128)(2,1)S(1)}, bf16[256,384]{1,0:T(8,128)(2,1)S(1)}, u32[]{:S(2)}, u32[]{:S(2)}) %collective-permute-start.3) | collective-permute-done | bytes 196640 | tf_op jit(solution)/shard_map/ppermute | solution.py:35
  84.1 0.0 collective-permute-done.2.refs_1_
  84.1 2.2 %weight_gradients.1 = (bf16[1536,384]{1,0:T(8,128)(2,1)}, bf16[384,1536]{1,0:T(8,128)(2,1)}) custom-call(bf16[256,1536]{1,0:T(8,128)(2,1)S(1)} %bitcast.9, bf16[256,1536]{1,0:T(8,128)(2,1)S(1)} %collective-permute-done.2.refs_1_, bf16[256,384]{1,0:T(8,128)(2,1)S(1)} %get-tuple-element.15.refs_2_, bf16[256,384]{1,0:T(8,128)(2,1)S(1)} %collective-permute-done.3.refs_3_), custom_call_target="tpu_custom_call" | custom-call | flops 603979776 | bytes 4325376 | tf_op jit(solution)/shard_map/weight_gradients/pallas_call | solution.py:45
  86.3 11.0 %all-to-all-done.4 = bf16[32,8,1536]{2,1,0:T(8,128)(2,1)S(1)} async-done(((bf16[32,8,1536]{2,1,0:T(8,128)(2,1)}), bf16[32,8,1536]{2,1,0:T(8,128)(2,1)S(1)}, u32[]{:S(2)}, u32[]{:S(2)}) %all-to-all-start.4) | async-done | bytes 786464 | tf_op jit(solution)/shard_map/all_to_all | solution.py:39
  97.3 0.1 reduce_sum.12
  97.4 0.6 fusion.1
  (1 shorter events, 0.0 us)
Async XLA Ops:
  2.1 19.0 %all-to-all-start = ((bf16[8,8,1536]{2,1,0:T(8,128)(2,1)}), bf16[8,8,1536]{2,1,0:T(8,128)(2,1)S(1)}, u32[]{:S(2)}, u32[]{:S(2)}) async-start(bf16[8,8,1536]{2,1,0:T(8,128)(2,1)} %broadcast_in_dim.2), calls=%async_computation | async-start | bytes 393216 | tf_op jit(solution)/shard_map/all_to_all | solution.py:39
  12.0 23.5 %collective-permute-start = (bf16[1536,384]{1,0:T(8,128)(2,1)}, bf16[1536,384]{1,0:T(8,128)(2,1)S(1)}, u32[]{:S(2)}, u32[]{:S(2)}) collective-permute-start(bf16[1536,384]{1,0:T(8,128)(2,1)} %refs_1_.3), channel_id=1, source_target_pairs={{0,1},{1,0},{2,3},{3,2},{4,5},{5,4},{6,7},{7,6},{8,9},{9,8},{10,11... | collective-permute-start | bytes 3538952 | tf_op jit(solution)/shard_map/ppermute | solution.py:35
  13.9 21.6 %collective-permute-start.1 = (bf16[384,1536]{1,0:T(8,128)(2,1)}, bf16[384,1536]{1,0:T(8,128)(2,1)S(1)}, u32[]{:S(2)}, u32[]{:S(2)}) collective-permute-start(bf16[384,1536]{1,0:T(8,128)(2,1)} %refs_2_.3), channel_id=1, source_target_pairs={{0,1},{1,0},{2,3},{3,2},{4,5},{5,4},{6,7},{7,6},{8,9},{9,8},{10,11... | collective-permute-start | bytes 3538952 | tf_op jit(solution)/shard_map/ppermute | solution.py:35
  21.0 14.5 %copy-start.1 = (bf16[384,1536]{1,0:T(8,128)(2,1)S(1)}, bf16[384,1536]{1,0:T(8,128)(2,1)}, u32[]{:S(2)}) copy-start(bf16[384,1536]{1,0:T(8,128)(2,1)} %refs_2_.3) | copy-start | bytes 3538948
  21.1 14.4 %copy-start = (bf16[1536,384]{1,0:T(8,128)(2,1)S(1)}, bf16[1536,384]{1,0:T(8,128)(2,1)}, u32[]{:S(2)}) copy-start(bf16[1536,384]{1,0:T(8,128)(2,1)} %refs_1_.3) | copy-start | bytes 3538948
  72.0 25.3 %all-to-all-start.4 = ((bf16[32,8,1536]{2,1,0:T(8,128)(2,1)}), bf16[32,8,1536]{2,1,0:T(8,128)(2,1)S(1)}, u32[]{:S(2)}, u32[]{:S(2)}) async-start(bf16[32,8,1536]{2,1,0:T(8,128)(2,1)} %bitcast.12), calls=%async_computation.4 | async-start | bytes 1572864 | tf_op jit(solution)/shard_map/all_to_all | solution.py:39
  78.7 5.4 %collective-permute-start.2 = (bf16[256,1536]{1,0:T(8,128)(2,1)S(1)}, bf16[256,1536]{1,0:T(8,128)(2,1)S(1)}, u32[]{:S(2)}, u32[]{:S(2)}) collective-permute-start(bf16[256,1536]{1,0:T(8,128)(2,1)S(1)} %bitcast.8), channel_id=1, source_target_pairs={{0,1},{1,0},{2,3},{3,2},{4,5},{5,4},{6,7},{7,6},{8,9},{9,8},{10,11... | collective-permute-start | bytes 2359304 | tf_op jit(solution)/shard_map/ppermute | solution.py:35
  80.6 3.5 %collective-permute-start.3 = (bf16[256,384]{1,0:T(8,128)(2,1)S(1)}, bf16[256,384]{1,0:T(8,128)(2,1)S(1)}, u32[]{:S(2)}, u32[]{:S(2)}) collective-permute-start(bf16[256,384]{1,0:T(8,128)(2,1)S(1)} %get-tuple-element.14), channel_id=1, source_target_pairs={{0,1},{1,0},{2,3},{3,2},{4,5},{5,4},{6,7},{7,6},{8,9},{9,8},{10,11... | collective-permute-start | bytes 589832 | tf_op jit(solution)/shard_map/ppermute | solution.py:35

commit v7 on v6

--- a/solution.py
+++ b/solution.py
@@ -95,17 +95,16 @@
 
 def terms_kernel(lines, rows, acts_ref, in_ref, out_ref, in_far_ref, out_far_ref, terms_ref):
     tokens, cotangent = kinds_of(acts_ref, lines)
-    units = in_ref.shape[1]
     size = terms_ref.shape[0] // rows
     half = size // 2
-    for place, (w_in, w_out) in enumerate(((in_ref, out_ref), (in_far_ref, out_far_ref))):
-        columns = slice(place * units, (place + 1) * units)
-        made = (contract(tokens, w_in[...], 1, 0), contract(cotangent, w_out[...], 1, 1))
-        for kind, term in enumerate(made):
-            term = term.astype(bf16)
-            for row in range(rows):
-                start = row * size + kind * half
-                terms_ref[start : start + half, columns] = term[row * half : (row + 1) * half]
+    w_in = jnp.concatenate([in_ref[...], in_far_ref[...]], axis=1)
+    w_out = jnp.concatenate([out_ref[...], out_far_ref[...]], axis=0)
+    made = (contract(tokens, w_in, 1, 0), contract(cotangent, w_out, 1, 1))
+    for kind, term in enumerate(made):
+        term = term.astype(bf16)
+        for row in range(rows):
+            start = row * size + kind * half
+            terms_ref[start : start + half] = term[row * half : (row + 1) * half]
 
 
 def gelu_kernel(terms_ref, out_ref):
@@ -122,17 +121,15 @@
 def sums_kernel(
     share, rows, made_ref, in_ref, out_ref, in_far_ref, out_far_ref, sums_hbm, sums_ref, sems
 ):
-    units, width = out_ref.shape
+    width = out_ref.shape[1]
     active, grads = kinds_of(made_ref, rows)
     group = 2 * share
     step = 512
     stores = []
     for place, start in enumerate(range(0, width, step)):
         part = slice(start, start + step)
-        ahead = contract(active[:, :units], out_ref[:, part], 1, 0)
-        ahead = ahead + contract(active[:, units:], out_far_ref[:, part], 1, 0)
-        back = contract(grads[:, :units], in_ref[part, :], 1, 1)
-        back = back + contract(grads[:, units:], in_far_ref[part, :], 1, 1)
+        ahead = contract(active, jnp.concatenate([out_ref[:, part], out_far_ref[:, part]], 0), 1, 0)
+        back = contract(grads, jnp.concatenate([in_ref[part, :], in_far_ref[part, :]], 1), 1, 1)
         ahead, back = (sums.reshape(-1, group, step) for sums in (ahead, back))
         even, odd = meet(ahead, turned(back), group), meet(turned(ahead), back, group)
         picked = jnp.stack([even, odd], axis=1).reshape(-1, step)

time: 98.6 us -> 98.5 us (level)
  no operation moved by 1% of the time
where the time goes in v7:
time: 98.5 us; the launch traced here: 98 us
  blocking collectives  47.4 us (48%)
  starting transfers between devices  25.3 us (26%)
  waiting for transfers between devices  16.7 us (17%)
  Pallas kernels  5.57 us (6%)
  local copies, waits for them, and re-layouts  1.36 us (1%)
    all_to_all x3, blocking collectives, exchange(): return lax.all_to_all(blocks, axes, split_axis=0, concat_axis=0)  47.4 us
    all_to_all x2, starting transfers between devices, exchange(): return lax.all_to_all(blocks, axes, split_axis=0, concat_axis=0)  16.6 us
    all_to_all x2, waiting for transfers between devices, exchange(): return lax.all_to_all(blocks, axes, split_axis=0, concat_axis=0)  15.7 us
    ppermute x4, starting transfers between devices, other_core(): return lax.ppermute(block, 'core', [(0, 1), (1, 0)])  8.65 us
    pallas_call x5, Pallas kernels, whole(): pl.pallas_call(kernel, out_shape=out_shapes, in_specs=[in_vmem] * len(arg...  5.57 us
  transfers between devices with their start and end apart: 6, of which 3 were waited for; matrix products, arithmetic and copies ran while one was open for 0% of the time, Pallas kernels for 2%

profile of v7, /device:TPU:64, one launch (start us, length us, event | category | flops | bytes accessed | tf_op | source)
XLA Modules:
  0.0 98.0 jit_solution(13151104397027291573)
XLA Ops:
  0.6 0.7 pad_maximum_fusion
  1.4 0.7 broadcast_in_dim.2
  2.1 10.0 %all-to-all-start = ((bf16[8,8,1536]{2,1,0:T(8,128)(2,1)}), bf16[8,8,1536]{2,1,0:T(8,128)(2,1)S(1)}, u32[]{:S(2)}, u32[]{:S(2)}) async-start(bf16[8,8,1536]{2,1,0:T(8,128)(2,1)} %broadcast_in_dim.2), calls=%async_computation | async-start | bytes 393216 | tf_op jit(solution)/shard_map/all_to_all | solution.py:39
  12.0 1.9 %collective-permute-start = (bf16[1536,384]{1,0:T(8,128)(2,1)}, bf16[1536,384]{1,0:T(8,128)(2,1)S(1)}, u32[]{:S(2)}, u32[]{:S(2)}) collective-permute-start(bf16[1536,384]{1,0:T(8,128)(2,1)} %refs_1_.3), channel_id=1, source_target_pairs={{0,1},{1,0},{2,3},{3,2},{4,5},{5,4},{6,7},{7,6},{8,9},{9,8},{10,11... | collective-permute-start | bytes 3538952 | tf_op jit(solution)/shard_map/ppermute | solution.py:35
  13.9 2.4 %collective-permute-start.1 = (bf16[384,1536]{1,0:T(8,128)(2,1)}, bf16[384,1536]{1,0:T(8,128)(2,1)S(1)}, u32[]{:S(2)}, u32[]{:S(2)}) collective-permute-start(bf16[384,1536]{1,0:T(8,128)(2,1)} %refs_2_.3), channel_id=1, source_target_pairs={{0,1},{1,0},{2,3},{3,2},{4,5},{5,4},{6,7},{7,6},{8,9},{9,8},{10,11... | collective-permute-start | bytes 3538952 | tf_op jit(solution)/shard_map/ppermute | solution.py:35
  16.4 4.7 %all-to-all-done = bf16[8,8,1536]{2,1,0:T(8,128)(2,1)S(1)} async-done(((bf16[8,8,1536]{2,1,0:T(8,128)(2,1)}), bf16[8,8,1536]{2,1,0:T(8,128)(2,1)S(1)}, u32[]{:S(2)}, u32[]{:S(2)}) %all-to-all-start) | async-done | bytes 196640 | tf_op jit(solution)/shard_map/all_to_all | solution.py:39
  21.0 0.0 copy-start.1
  21.1 0.1 spread_rows.1
  21.1 0.0 copy-start
  21.1 14.4 %all_to_all.25 = bf16[4,64,1536]{2,1,0:T(8,128)(2,1)S(1)} all-to-all(bf16[4,64,1536]{2,1,0:T(8,128)(2,1)S(1)} %spread_rows.1), channel_id=1, replica_groups=mesh['row'=8,'col'=8,'x'=4,'core'=2] {'x'}, dimensions={0} | all-to-all | bytes 1572864 | tf_op jit(solution)/shard_map/all_to_all | solution.py:39
  35.5 0.0 collective-permute-done.refs_3_
  35.5 0.0 collective-permute-done.1.refs_4_
  35.5 0.0 copy-done.1
  35.5 0.0 copy-done
  35.5 1.2 %hidden_terms.1 = bf16[256,768]{1,0:T(8,128)(2,1)S(1)} custom-call(bf16[256,1536]{1,0:T(8,128)(2,1)S(1)} %bitcast.7, bf16[1536,384]{1,0:T(8,128)(2,1)S(1)} %copy-done, bf16[384,1536]{1,0:T(8,128)(2,1)S(1)} %copy-done.1, bf16[1536,384]{1,0:T(8,128)(2,1)S(1)} %collective-permute-done.refs_3_, bf16[384,1536]{1,0:T(8,128)(2,1)S(1)} %collective-permute-done.1.refs_4_), custom_call_target="tpu_custom_call" | custom-call | flops 603979776 | bytes 5898240 | tf_op jit(solution)/shard_map/hidden_terms/pallas_call | solution.py:45
  36.7 18.8 %all_to_all.26.terms_ref = bf16[8,32,768]{2,1,0:T(8,128)(2,1)S(1)} all-to-all(bf16[8,32,768]{2,1,0:T(8,128)(2,1)S(1)} %bitcast.10), channel_id=1, replica_groups=mesh['row'=8,'col'=8,'x'=4,'core'=2] {'row'}, dimensions={0} | all-to-all | bytes 786432 | tf_op jit(solution)/shard_map/all_to_all | solution.py:39
  55.5 0.1 gelu_rows.1
  55.6 14.3 %all_to_all.27 = bf16[8,32,768]{2,1,0:T(8,128)(2,1)S(1)} all-to-all(bf16[8,32,768]{2,1,0:T(8,128)(2,1)S(1)} %gelu_rows.1), channel_id=1, replica_groups=mesh['row'=8,'col'=8,'x'=4,'core'=2] {'row'}, dimensions={0} | all-to-all | bytes 786432 | tf_op jit(solution)/shard_map/all_to_all | solution.py:39
  69.9 2.0 %output_terms.1 = bf16[256,1536]{1,0:T(8,128)(2,1)} custom-call(bf16[256,768]{1,0:T(8,128)(2,1)S(1)} %bitcast.5, bf16[1536,384]{1,0:T(8,128)(2,1)S(1)} %copy-done, bf16[384,1536]{1,0:T(8,128)(2,1)S(1)} %copy-done.1, bf16[1536,384]{1,0:T(8,128)(2,1)S(1)} %collective-permute-done.refs_3_, bf16[384,1536]{1,0:T(8,128)(2,1)S(1)} %collective-permute-done.1.refs_4_), custom_call_target="tpu_custom_call" | custom-call | flops 603979776 | bytes 5898240 | tf_op jit(solution)/shard_map/output_terms/pallas_call | solution.py:45
  71.9 6.7 %all-to-all-start.4 = ((bf16[32,8,1536]{2,1,0:T(8,128)(2,1)}), bf16[32,8,1536]{2,1,0:T(8,128)(2,1)S(1)}, u32[]{:S(2)}, u32[]{:S(2)}) async-start(bf16[32,8,1536]{2,1,0:T(8,128)(2,1)} %bitcast.12), calls=%async_computation.4 | async-start | bytes 1572864 | tf_op jit(solution)/shard_map/all_to_all | solution.py:39
  78.6 1.9 %collective-permute-start.2 = (bf16[256,1536]{1,0:T(8,128)(2,1)S(1)}, bf16[256,1536]{1,0:T(8,128)(2,1)S(1)}, u32[]{:S(2)}, u32[]{:S(2)}) collective-permute-start(bf16[256,1536]{1,0:T(8,128)(2,1)S(1)} %bitcast.8), channel_id=1, source_target_pairs={{0,1},{1,0},{2,3},{3,2},{4,5},{5,4},{6,7},{7,6},{8,9},{9,8},{10,11... | collective-permute-start | bytes 2359304 | tf_op jit(solution)/shard_map/ppermute | solution.py:35
  80.6 2.4 %collective-permute-start.3 = (bf16[256,384]{1,0:T(8,128)(2,1)S(1)}, bf16[256,384]{1,0:T(8,128)(2,1)S(1)}, u32[]{:S(2)}, u32[]{:S(2)}) collective-permute-start(bf16[256,384]{1,0:T(8,128)(2,1)S(1)} %get-tuple-element.14), channel_id=1, source_target_pairs={{0,1},{1,0},{2,3},{3,2},{4,5},{5,4},{6,7},{7,6},{8,9},{9,8},{10,11... | collective-permute-start | bytes 589832 | tf_op jit(solution)/shard_map/ppermute | solution.py:35
  83.0 1.0 %collective-permute-done.3.refs_3_ = bf16[256,384]{1,0:T(8,128)(2,1)S(1)} collective-permute-done((bf16[256,384]{1,0:T(8,128)(2,1)S(1)}, bf16[256,384]{1,0:T(8,128)(2,1)S(1)}, u32[]{:S(2)}, u32[]{:S(2)}) %collective-permute-start.3) | collective-permute-done | bytes 196640 | tf_op jit(solution)/shard_map/ppermute | solution.py:35
  84.0 0.0 collective-permute-done.2.refs_1_
  84.0 2.2 %weight_gradients.1 = (bf16[1536,384]{1,0:T(8,128)(2,1)}, bf16[384,1536]{1,0:T(8,128)(2,1)}) custom-call(bf16[256,1536]{1,0:T(8,128)(2,1)S(1)} %bitcast.9, bf16[256,1536]{1,0:T(8,128)(2,1)S(1)} %collective-permute-done.2.refs_1_, bf16[256,384]{1,0:T(8,128)(2,1)S(1)} %get-tuple-element.15.refs_2_, bf16[256,384]{1,0:T(8,128)(2,1)S(1)} %collective-permute-done.3.refs_3_), custom_call_target="tpu_custom_call" | custom-call | flops 603979776 | bytes 4325376 | tf_op jit(solution)/shard_map/weight_gradients/pallas_call | solution.py:45
  86.2 11.0 %all-to-all-done.4 = bf16[32,8,1536]{2,1,0:T(8,128)(2,1)S(1)} async-done(((bf16[32,8,1536]{2,1,0:T(8,128)(2,1)}), bf16[32,8,1536]{2,1,0:T(8,128)(2,1)S(1)}, u32[]{:S(2)}, u32[]{:S(2)}) %all-to-all-start.4) | async-done | bytes 786464 | tf_op jit(solution)/shard_map/all_to_all | solution.py:39
  97.2 0.1 reduce_sum.12
  97.3 0.6 fusion.1
  (1 shorter events, 0.0 us)
Async XLA Ops:
  2.1 19.0 %all-to-all-start = ((bf16[8,8,1536]{2,1,0:T(8,128)(2,1)}), bf16[8,8,1536]{2,1,0:T(8,128)(2,1)S(1)}, u32[]{:S(2)}, u32[]{:S(2)}) async-start(bf16[8,8,1536]{2,1,0:T(8,128)(2,1)} %broadcast_in_dim.2), calls=%async_computation | async-start | bytes 393216 | tf_op jit(solution)/shard_map/all_to_all | solution.py:39
  12.0 23.5 %collective-permute-start = (bf16[1536,384]{1,0:T(8,128)(2,1)}, bf16[1536,384]{1,0:T(8,128)(2,1)S(1)}, u32[]{:S(2)}, u32[]{:S(2)}) collective-permute-start(bf16[1536,384]{1,0:T(8,128)(2,1)} %refs_1_.3), channel_id=1, source_target_pairs={{0,1},{1,0},{2,3},{3,2},{4,5},{5,4},{6,7},{7,6},{8,9},{9,8},{10,11... | collective-permute-start | bytes 3538952 | tf_op jit(solution)/shard_map/ppermute | solution.py:35
  13.9 21.6 %collective-permute-start.1 = (bf16[384,1536]{1,0:T(8,128)(2,1)}, bf16[384,1536]{1,0:T(8,128)(2,1)S(1)}, u32[]{:S(2)}, u32[]{:S(2)}) collective-permute-start(bf16[384,1536]{1,0:T(8,128)(2,1)} %refs_2_.3), channel_id=1, source_target_pairs={{0,1},{1,0},{2,3},{3,2},{4,5},{5,4},{6,7},{7,6},{8,9},{9,8},{10,11... | collective-permute-start | bytes 3538952 | tf_op jit(solution)/shard_map/ppermute | solution.py:35
  21.0 14.5 %copy-start.1 = (bf16[384,1536]{1,0:T(8,128)(2,1)S(1)}, bf16[384,1536]{1,0:T(8,128)(2,1)}, u32[]{:S(2)}) copy-start(bf16[384,1536]{1,0:T(8,128)(2,1)} %refs_2_.3) | copy-start | bytes 3538948
  21.1 14.4 %copy-start = (bf16[1536,384]{1,0:T(8,128)(2,1)S(1)}, bf16[1536,384]{1,0:T(8,128)(2,1)}, u32[]{:S(2)}) copy-start(bf16[1536,384]{1,0:T(8,128)(2,1)} %refs_1_.3) | copy-start | bytes 3538948
  71.9 25.3 %all-to-all-start.4 = ((bf16[32,8,1536]{2,1,0:T(8,128)(2,1)}), bf16[32,8,1536]{2,1,0:T(8,128)(2,1)S(1)}, u32[]{:S(2)}, u32[]{:S(2)}) async-start(bf16[32,8,1536]{2,1,0:T(8,128)(2,1)} %bitcast.12), calls=%async_computation.4 | async-start | bytes 1572864 | tf_op jit(solution)/shard_map/all_to_all | solution.py:39
  78.6 5.4 %collective-permute-start.2 = (bf16[256,1536]{1,0:T(8,128)(2,1)S(1)}, bf16[256,1536]{1,0:T(8,128)(2,1)S(1)}, u32[]{:S(2)}, u32[]{:S(2)}) collective-permute-start(bf16[256,1536]{1,0:T(8,128)(2,1)S(1)} %bitcast.8), channel_id=1, source_target_pairs={{0,1},{1,0},{2,3},{3,2},{4,5},{5,4},{6,7},{7,6},{8,9},{9,8},{10,11... | collective-permute-start | bytes 2359304 | tf_op jit(solution)/shard_map/ppermute | solution.py:35
  80.6 3.5 %collective-permute-start.3 = (bf16[256,384]{1,0:T(8,128)(2,1)S(1)}, bf16[256,384]{1,0:T(8,128)(2,1)S(1)}, u32[]{:S(2)}, u32[]{:S(2)}) collective-permute-start(bf16[256,384]{1,0:T(8,128)(2,1)S(1)} %get-tuple-element.14), channel_id=1, source_target_pairs={{0,1},{1,0},{2,3},{3,2},{4,5},{5,4},{6,7},{7,6},{8,9},{9,8},{10,11... | collective-permute-start | bytes 589832 | tf_op jit(solution)/shard_map/ppermute | solution.py:35

commit v8 on v6

--- a/solution.py
+++ b/solution.py
@@ -212,7 +212,8 @@
     final = jnp.sum(blocks.astype(f32), axis=0).astype(bf16)
 
     made_far = other_core(made[:, units:])
-    acts_far = other_core(acts)
+    made_far, waiting = lax.optimization_barrier((made_far, acts))
+    acts_far = other_core(waiting)
     grad_weight_in, grad_weight_out = whole(
         bind(weight_kernel, xs, rows),
         "weight_gradients",

time: 98.6 us -> 98.6 us (level)
    ppermute x4, waiting for transfers between devices: 1.06 us -> 3.54 us  [other_core(): return lax.ppermute(block, 'core', [(0, 1), (1, 0)])]
    all_to_all x2, waiting for transfers between devices: 15.7 us -> 13.5 us  [exchange(): return lax.all_to_all(blocks, axes, split_axis=0, concat_axis=0)]
  transfers between devices with their start and end apart: 6 -> 6, of which waited for: 3 -> 4; matrix products, arithmetic and copies ran while one was open for 0% -> 0% of each run, Pallas kernels for 2% -> 2%
where the time goes in v8:
time: 98.6 us; the launch traced here: 98 us
  blocking collectives  47.4 us (48%)
  starting transfers between devices  24.9 us (25%)
  waiting for transfers between devices  17.1 us (17%)
  Pallas kernels  5.64 us (6%)
  local copies, waits for them, and re-layouts  1.36 us (1%)
    all_to_all x3, blocking collectives, exchange(): return lax.all_to_all(blocks, axes, split_axis=0, concat_axis=0)  47.4 us
    all_to_all x2, starting transfers between devices, exchange(): return lax.all_to_all(blocks, axes, split_axis=0, concat_axis=0)  16.6 us
    all_to_all x2, waiting for transfers between devices, exchange(): return lax.all_to_all(blocks, axes, split_axis=0, concat_axis=0)  13.5 us
    ppermute x4, starting transfers between devices, other_core(): return lax.ppermute(block, 'core', [(0, 1), (1, 0)])  8.27 us
    pallas_call x5, Pallas kernels, whole(): pl.pallas_call(kernel, out_shape=out_shapes, in_specs=[in_vmem] * len(arg...  5.64 us
    ppermute x4, waiting for transfers between devices, other_core(): return lax.ppermute(block, 'core', [(0, 1), (1, 0)])  3.54 us
  transfers between devices with their start and end apart: 6, of which 4 were waited for; matrix products, arithmetic and copies ran while one was open for 0% of the time, Pallas kernels for 2%

profile of v8, /device:TPU:64, one launch (start us, length us, event | category | flops | bytes accessed | tf_op | source)
XLA Modules:
  0.0 98.0 jit_solution(9969953879225202536)
XLA Ops:
  0.6 0.7 pad_maximum_fusion
  1.4 0.7 broadcast_in_dim.2
  2.1 10.0 %all-to-all-start = ((bf16[8,8,1536]{2,1,0:T(8,128)(2,1)}), bf16[8,8,1536]{2,1,0:T(8,128)(2,1)S(1)}, u32[]{:S(2)}, u32[]{:S(2)}) async-start(bf16[8,8,1536]{2,1,0:T(8,128)(2,1)} %broadcast_in_dim.2), calls=%async_computation | async-start | bytes 393216 | tf_op jit(solution)/shard_map/all_to_all | solution.py:39
  12.0 1.9 %collective-permute-start = (bf16[1536,384]{1,0:T(8,128)(2,1)}, bf16[1536,384]{1,0:T(8,128)(2,1)S(1)}, u32[]{:S(2)}, u32[]{:S(2)}) collective-permute-start(bf16[1536,384]{1,0:T(8,128)(2,1)} %refs_1_.3), channel_id=1, source_target_pairs={{0,1},{1,0},{2,3},{3,2},{4,5},{5,4},{6,7},{7,6},{8,9},{9,8},{10,11... | collective-permute-start | bytes 3538952 | tf_op jit(solution)/shard_map/ppermute | solution.py:35
  13.9 2.4 %collective-permute-start.1 = (bf16[384,1536]{1,0:T(8,128)(2,1)}, bf16[384,1536]{1,0:T(8,128)(2,1)S(1)}, u32[]{:S(2)}, u32[]{:S(2)}) collective-permute-start(bf16[384,1536]{1,0:T(8,128)(2,1)} %refs_2_.3), channel_id=1, source_target_pairs={{0,1},{1,0},{2,3},{3,2},{4,5},{5,4},{6,7},{7,6},{8,9},{9,8},{10,11... | collective-permute-start | bytes 3538952 | tf_op jit(solution)/shard_map/ppermute | solution.py:35
  16.4 4.7 %all-to-all-done = bf16[8,8,1536]{2,1,0:T(8,128)(2,1)S(1)} async-done(((bf16[8,8,1536]{2,1,0:T(8,128)(2,1)}), bf16[8,8,1536]{2,1,0:T(8,128)(2,1)S(1)}, u32[]{:S(2)}, u32[]{:S(2)}) %all-to-all-start) | async-done | bytes 196640 | tf_op jit(solution)/shard_map/all_to_all | solution.py:39
  21.0 0.0 copy-start.1
  21.1 0.1 spread_rows.1
  21.1 0.0 copy-start
  21.1 14.4 %all_to_all.25 = bf16[4,64,1536]{2,1,0:T(8,128)(2,1)S(1)} all-to-all(bf16[4,64,1536]{2,1,0:T(8,128)(2,1)S(1)} %spread_rows.1), channel_id=1, replica_groups=mesh['row'=8,'col'=8,'x'=4,'core'=2] {'x'}, dimensions={0} | all-to-all | bytes 1572864 | tf_op jit(solution)/shard_map/all_to_all | solution.py:39
  35.5 0.0 collective-permute-done.refs_3_
  35.5 0.0 collective-permute-done.1.refs_4_
  35.5 0.0 copy-done.1
  35.5 0.0 copy-done
  35.5 1.2 %hidden_terms.1 = bf16[256,768]{1,0:T(8,128)(2,1)S(1)} custom-call(bf16[256,1536]{1,0:T(8,128)(2,1)S(1)} %bitcast.7, bf16[1536,384]{1,0:T(8,128)(2,1)S(1)} %copy-done, bf16[384,1536]{1,0:T(8,128)(2,1)S(1)} %copy-done.1, bf16[1536,384]{1,0:T(8,128)(2,1)S(1)} %collective-permute-done.refs_3_, bf16[384,1536]{1,0:T(8,128)(2,1)S(1)} %collective-permute-done.1.refs_4_), custom_call_target="tpu_custom_call" | custom-call | flops 603979776 | bytes 5898240 | tf_op jit(solution)/shard_map/hidden_terms/pallas_call | solution.py:45
  36.8 18.8 %all_to_all.26.terms_ref = bf16[8,32,768]{2,1,0:T(8,128)(2,1)S(1)} all-to-all(bf16[8,32,768]{2,1,0:T(8,128)(2,1)S(1)} %bitcast.10), channel_id=1, replica_groups=mesh['row'=8,'col'=8,'x'=4,'core'=2] {'row'}, dimensions={0} | all-to-all | bytes 786432 | tf_op jit(solution)/shard_map/all_to_all | solution.py:39
  55.5 0.1 gelu_rows.1
  55.6 14.3 %all_to_all.27 = bf16[8,32,768]{2,1,0:T(8,128)(2,1)S(1)} all-to-all(bf16[8,32,768]{2,1,0:T(8,128)(2,1)S(1)} %gelu_rows.1), channel_id=1, replica_groups=mesh['row'=8,'col'=8,'x'=4,'core'=2] {'row'}, dimensions={0} | all-to-all | bytes 786432 | tf_op jit(solution)/shard_map/all_to_all | solution.py:39
  69.9 2.1 %output_terms.1 = bf16[256,1536]{1,0:T(8,128)(2,1)} custom-call(bf16[256,768]{1,0:T(8,128)(2,1)S(1)} %bitcast.5, bf16[1536,384]{1,0:T(8,128)(2,1)S(1)} %copy-done, bf16[384,1536]{1,0:T(8,128)(2,1)S(1)} %copy-done.1, bf16[1536,384]{1,0:T(8,128)(2,1)S(1)} %collective-permute-done.refs_3_, bf16[384,1536]{1,0:T(8,128)(2,1)S(1)} %collective-permute-done.1.refs_4_), custom_call_target="tpu_custom_call" | custom-call | flops 603979776 | bytes 5898240 | tf_op jit(solution)/shard_map/output_terms/pallas_call | solution.py:45
  72.0 6.7 %all-to-all-start.4 = ((bf16[32,8,1536]{2,1,0:T(8,128)(2,1)}), bf16[32,8,1536]{2,1,0:T(8,128)(2,1)S(1)}, u32[]{:S(2)}, u32[]{:S(2)}) async-start(bf16[32,8,1536]{2,1,0:T(8,128)(2,1)} %bitcast.12), calls=%async_computation.4 | async-start | bytes 1572864 | tf_op jit(solution)/shard_map/all_to_all | solution.py:39
  78.7 1.9 %collective-permute-start.2 = (bf16[256,384]{1,0:T(8,128)(2,1)S(1)}, bf16[256,384]{1,0:T(8,128)(2,1)S(1)}, u32[]{:S(2)}, u32[]{:S(2)}) collective-permute-start(bf16[256,384]{1,0:T(8,128)(2,1)S(1)} %get-tuple-element.19), channel_id=1, source_target_pairs={{0,1},{1,0},{2,3},{3,2},{4,5},{5,4},{6,7},{7,6},{8,9},{9,8},{10,11... | collective-permute-start | bytes 589832 | tf_op jit(solution)/shard_map/ppermute | solution.py:35
  80.6 1.4 %collective-permute-done.2.refs_3_ = bf16[256,384]{1,0:T(8,128)(2,1)S(1)} collective-permute-done((bf16[256,384]{1,0:T(8,128)(2,1)S(1)}, bf16[256,384]{1,0:T(8,128)(2,1)S(1)}, u32[]{:S(2)}, u32[]{:S(2)}) %collective-permute-start.2) | collective-permute-done | bytes 196640 | tf_op jit(solution)/shard_map/ppermute | solution.py:35
  82.0 2.0 %collective-permute-start.3 = (bf16[256,1536]{1,0:T(8,128)(2,1)S(1)}, bf16[256,1536]{1,0:T(8,128)(2,1)S(1)}, u32[]{:S(2)}, u32[]{:S(2)}) collective-permute-start(bf16[256,1536]{1,0:T(8,128)(2,1)S(1)} %bitcast.8), channel_id=1, source_target_pairs={{0,1},{1,0},{2,3},{3,2},{4,5},{5,4},{6,7},{7,6},{8,9},{9,8},{10,11... | collective-permute-start | bytes 2359304 | tf_op jit(solution)/shard_map/ppermute | solution.py:35
  84.1 2.1 %collective-permute-done.3.refs_1_ = bf16[256,1536]{1,0:T(8,128)(2,1)S(1)} collective-permute-done((bf16[256,1536]{1,0:T(8,128)(2,1)S(1)}, bf16[256,1536]{1,0:T(8,128)(2,1)S(1)}, u32[]{:S(2)}, u32[]{:S(2)}) %collective-permute-start.3) | collective-permute-done | bytes 786464 | tf_op jit(solution)/shard_map/ppermute | solution.py:35
  86.2 2.2 %weight_gradients.1 = (bf16[1536,384]{1,0:T(8,128)(2,1)}, bf16[384,1536]{1,0:T(8,128)(2,1)}) custom-call(bf16[256,1536]{1,0:T(8,128)(2,1)S(1)} %bitcast.9, bf16[256,1536]{1,0:T(8,128)(2,1)S(1)} %collective-permute-done.3.refs_1_, bf16[256,384]{1,0:T(8,128)(2,1)S(1)} %get-tuple-element.18.refs_2_, bf16[256,384]{1,0:T(8,128)(2,1)S(1)} %collective-permute-done.2.refs_3_), custom_call_target="tpu_custom_call" | custom-call | flops 603979776 | bytes 4325376 | tf_op jit(solution)/shard_map/weight_gradients/pallas_call | solution.py:45
  88.4 8.9 %all-to-all-done.4 = bf16[32,8,1536]{2,1,0:T(8,128)(2,1)S(1)} async-done(((bf16[32,8,1536]{2,1,0:T(8,128)(2,1)}), bf16[32,8,1536]{2,1,0:T(8,128)(2,1)S(1)}, u32[]{:S(2)}, u32[]{:S(2)}) %all-to-all-start.4) | async-done | bytes 786464 | tf_op jit(solution)/shard_map/all_to_all | solution.py:39
  97.3 0.1 reduce_sum.12
  97.4 0.6 fusion.1
  (1 shorter events, 0.0 us)
Async XLA Ops:
  2.1 19.0 %all-to-all-start = ((bf16[8,8,1536]{2,1,0:T(8,128)(2,1)}), bf16[8,8,1536]{2,1,0:T(8,128)(2,1)S(1)}, u32[]{:S(2)}, u32[]{:S(2)}) async-start(bf16[8,8,1536]{2,1,0:T(8,128)(2,1)} %broadcast_in_dim.2), calls=%async_computation | async-start | bytes 393216 | tf_op jit(solution)/shard_map/all_to_all | solution.py:39
  12.0 23.5 %collective-permute-start = (bf16[1536,384]{1,0:T(8,128)(2,1)}, bf16[1536,384]{1,0:T(8,128)(2,1)S(1)}, u32[]{:S(2)}, u32[]{:S(2)}) collective-permute-start(bf16[1536,384]{1,0:T(8,128)(2,1)} %refs_1_.3), channel_id=1, source_target_pairs={{0,1},{1,0},{2,3},{3,2},{4,5},{5,4},{6,7},{7,6},{8,9},{9,8},{10,11... | collective-permute-start | bytes 3538952 | tf_op jit(solution)/shard_map/ppermute | solution.py:35
  13.9 21.6 %collective-permute-start.1 = (bf16[384,1536]{1,0:T(8,128)(2,1)}, bf16[384,1536]{1,0:T(8,128)(2,1)S(1)}, u32[]{:S(2)}, u32[]{:S(2)}) collective-permute-start(bf16[384,1536]{1,0:T(8,128)(2,1)} %refs_2_.3), channel_id=1, source_target_pairs={{0,1},{1,0},{2,3},{3,2},{4,5},{5,4},{6,7},{7,6},{8,9},{9,8},{10,11... | collective-permute-start | bytes 3538952 | tf_op jit(solution)/shard_map/ppermute | solution.py:35
  21.0 14.5 %copy-start.1 = (bf16[384,1536]{1,0:T(8,128)(2,1)S(1)}, bf16[384,1536]{1,0:T(8,128)(2,1)}, u32[]{:S(2)}) copy-start(bf16[384,1536]{1,0:T(8,128)(2,1)} %refs_2_.3) | copy-start | bytes 3538948
  21.1 14.4 %copy-start = (bf16[1536,384]{1,0:T(8,128)(2,1)S(1)}, bf16[1536,384]{1,0:T(8,128)(2,1)}, u32[]{:S(2)}) copy-start(bf16[1536,384]{1,0:T(8,128)(2,1)} %refs_1_.3) | copy-start | bytes 3538948
  72.0 25.3 %all-to-all-start.4 = ((bf16[32,8,1536]{2,1,0:T(8,128)(2,1)}), bf16[32,8,1536]{2,1,0:T(8,128)(2,1)S(1)}, u32[]{:S(2)}, u32[]{:S(2)}) async-start(bf16[32,8,1536]{2,1,0:T(8,128)(2,1)} %bitcast.12), calls=%async_computation.4 | async-start | bytes 1572864 | tf_op jit(solution)/shard_map/all_to_all | solution.py:39
  78.7 3.3 %collective-permute-start.2 = (bf16[256,384]{1,0:T(8,128)(2,1)S(1)}, bf16[256,384]{1,0:T(8,128)(2,1)S(1)}, u32[]{:S(2)}, u32[]{:S(2)}) collective-permute-start(bf16[256,384]{1,0:T(8,128)(2,1)S(1)} %get-tuple-element.19), channel_id=1, source_target_pairs={{0,1},{1,0},{2,3},{3,2},{4,5},{5,4},{6,7},{7,6},{8,9},{9,8},{10,11... | collective-permute-start | bytes 589832 | tf_op jit(solution)/shard_map/ppermute | solution.py:35
  82.0 4.2 %collective-permute-start.3 = (bf16[256,1536]{1,0:T(8,128)(2,1)S(1)}, bf16[256,1536]{1,0:T(8,128)(2,1)S(1)}, u32[]{:S(2)}, u32[]{:S(2)}) collective-permute-start(bf16[256,1536]{1,0:T(8,128)(2,1)S(1)} %bitcast.8), channel_id=1, source_target_pairs={{0,1},{1,0},{2,3},{3,2},{4,5},{5,4},{6,7},{7,6},{8,9},{9,8},{10,11... | collective-permute-start | bytes 2359304 | tf_op jit(solution)/shard_map/ppermute | solution.py:35

commit v9 on v6

--- a/solution.py
+++ b/solution.py
@@ -175,7 +175,8 @@
 
     both = jnp.concatenate([tokens, cotangent], axis=0)
     weight_in_far = other_core(weight_in)
-    weight_out_far = other_core(weight_out)
+    weight_in_far, waiting = lax.optimization_barrier((weight_in_far, weight_out))
+    weight_out_far = other_core(waiting)
     weights = (weight_in, weight_out, weight_in_far, weight_out_far)
     cols, xs = lax.axis_size("col"), lax.axis_size("x")
     line = exchange(jnp.broadcast_to(both[None], (cols,) + both.shape), "col")
@@ -212,7 +213,8 @@
     final = jnp.sum(blocks.astype(f32), axis=0).astype(bf16)
 
     made_far = other_core(made[:, units:])
-    acts_far = other_core(acts)
+    made_far, held_acts = lax.optimization_barrier((made_far, acts))
+    acts_far = other_core(held_acts)
     grad_weight_in, grad_weight_out = whole(
         bind(weight_kernel, xs, rows),
         "weight_gradients",

time: 98.6 us -> 106 us (1.075)
  waiting for transfers between devices: 16.7 us -> 21.6 us
  starting transfers between devices: 25.3 us -> 27.2 us
    all_to_all x2, starting transfers between devices: 16.6 us -> 19.4 us  [exchange(): return lax.all_to_all(blocks, axes, split_axis=0, concat_axis=0)]
    ppermute x4, waiting for transfers between devices: 1.06 us -> 3.54 us  [other_core(): return lax.ppermute(block, 'core', [(0, 1), (1, 0)])]
    all_to_all x2, waiting for transfers between devices: 15.7 us -> 18.1 us  [exchange(): return lax.all_to_all(blocks, axes, split_axis=0, concat_axis=0)]
  transfers between devices with their start and end apart: 6 -> 6, of which waited for: 3 -> 4; matrix products, arithmetic and copies ran while one was open for 0% -> 1% of each run, Pallas kernels for 2% -> 2%
where the time goes in v9:
time: 106 us; the launch traced here: 105 us
  blocking collectives  48.1 us (45%)
  starting transfers between devices  27.2 us (26%)
  waiting for transfers between devices  21.6 us (20%)
  Pallas kernels  5.63 us (5%)
  local copies, waits for them, and re-layouts  1.36 us (1%)
    all_to_all x3, blocking collectives, exchange(): return lax.all_to_all(blocks, axes, split_axis=0, concat_axis=0)  48.1 us
    all_to_all x2, starting transfers between devices, exchange(): return lax.all_to_all(blocks, axes, split_axis=0, concat_axis=0)  19.4 us
    all_to_all x2, waiting for transfers between devices, exchange(): return lax.all_to_all(blocks, axes, split_axis=0, concat_axis=0)  18.1 us
    ppermute x4, starting transfers between devices, other_core(): return lax.ppermute(block, 'core', [(0, 1), (1, 0)])  7.79 us
    pallas_call x5, Pallas kernels, whole(): pl.pallas_call(kernel, out_shape=out_shapes, in_specs=[in_vmem] * len(arg...  5.63 us
    ppermute x4, waiting for transfers between devices, other_core(): return lax.ppermute(block, 'core', [(0, 1), (1, 0)])  3.54 us
  transfers between devices with their start and end apart: 6, of which 4 were waited for; matrix products, arithmetic and copies ran while one was open for 1% of the time, Pallas kernels for 2%

profile of v9, /device:TPU:64, one launch (start us, length us, event | category | flops | bytes accessed | tf_op | source)
XLA Modules:
  0.0 105.4 jit_solution(7081024632960017757)
XLA Ops:
  0.6 1.9 %collective-permute-start = (bf16[1536,384]{1,0:T(8,128)(2,1)}, bf16[1536,384]{1,0:T(8,128)(2,1)S(1)}, u32[]{:S(2)}, u32[]{:S(2)}) collective-permute-start(bf16[1536,384]{1,0:T(8,128)(2,1)} %refs_1_.3), channel_id=1, source_target_pairs={{0,1},{1,0},{2,3},{3,2},{4,5},{5,4},{6,7},{7,6},{8,9},{9,8},{10,11... | collective-permute-start | bytes 3538952 | tf_op jit(solution)/shard_map/ppermute | solution.py:35
  2.6 0.7 pad_maximum_fusion
  3.3 0.7 broadcast_in_dim.2
  4.0 10.0 %all-to-all-start = ((bf16[8,8,1536]{2,1,0:T(8,128)(2,1)}), bf16[8,8,1536]{2,1,0:T(8,128)(2,1)S(1)}, u32[]{:S(2)}, u32[]{:S(2)}) async-start(bf16[8,8,1536]{2,1,0:T(8,128)(2,1)} %broadcast_in_dim.2), calls=%async_computation | async-start | bytes 393216 | tf_op jit(solution)/shard_map/all_to_all | solution.py:39
  14.0 0.0 collective-permute-done.refs_3_
  14.0 1.9 %collective-permute-start.1 = (bf16[384,1536]{1,0:T(8,128)(2,1)}, bf16[384,1536]{1,0:T(8,128)(2,1)S(1)}, u32[]{:S(2)}, u32[]{:S(2)}) collective-permute-start(bf16[384,1536]{1,0:T(8,128)(2,1)} %refs_2_.3), channel_id=1, source_target_pairs={{0,1},{1,0},{2,3},{3,2},{4,5},{5,4},{6,7},{7,6},{8,9},{9,8},{10,11... | collective-permute-start | bytes 3538952 | tf_op jit(solution)/shard_map/ppermute | solution.py:35
  15.9 7.8 %all-to-all-done = bf16[8,8,1536]{2,1,0:T(8,128)(2,1)S(1)} async-done(((bf16[8,8,1536]{2,1,0:T(8,128)(2,1)}), bf16[8,8,1536]{2,1,0:T(8,128)(2,1)S(1)}, u32[]{:S(2)}, u32[]{:S(2)}) %all-to-all-start) | async-done | bytes 196640 | tf_op jit(solution)/shard_map/all_to_all | solution.py:39
  23.6 0.0 copy-start.1
  23.6 0.1 spread_rows.1
  23.7 0.0 copy-start
  23.7 14.9 %all_to_all.25 = bf16[4,64,1536]{2,1,0:T(8,128)(2,1)S(1)} all-to-all(bf16[4,64,1536]{2,1,0:T(8,128)(2,1)S(1)} %spread_rows.1), channel_id=1, replica_groups=mesh['row'=8,'col'=8,'x'=4,'core'=2] {'x'}, dimensions={0} | all-to-all | bytes 1572864 | tf_op jit(solution)/shard_map/all_to_all | solution.py:39
  38.6 0.0 collective-permute-done.1.refs_4_
  38.6 0.0 copy-done.1
  38.6 0.0 copy-done
  38.6 1.2 %hidden_terms.1 = bf16[256,768]{1,0:T(8,128)(2,1)S(1)} custom-call(bf16[256,1536]{1,0:T(8,128)(2,1)S(1)} %bitcast.7, bf16[1536,384]{1,0:T(8,128)(2,1)S(1)} %copy-done, bf16[384,1536]{1,0:T(8,128)(2,1)S(1)} %copy-done.1, bf16[1536,384]{1,0:T(8,128)(2,1)S(1)} %collective-permute-done.refs_3_, bf16[384,1536]{1,0:T(8,128)(2,1)S(1)} %collective-permute-done.1.refs_4_), custom_call_target="tpu_custom_call" | custom-call | flops 603979776 | bytes 5898240 | tf_op jit(solution)/shard_map/hidden_terms/pallas_call | solution.py:45
  39.9 18.9 %all_to_all.26.terms_ref = bf16[8,32,768]{2,1,0:T(8,128)(2,1)S(1)} all-to-all(bf16[8,32,768]{2,1,0:T(8,128)(2,1)S(1)} %bitcast.10), channel_id=1, replica_groups=mesh['row'=8,'col'=8,'x'=4,'core'=2] {'row'}, dimensions={0} | all-to-all | bytes 786432 | tf_op jit(solution)/shard_map/all_to_all | solution.py:39
  58.8 0.1 gelu_rows.1
  58.8 14.3 %all_to_all.27 = bf16[8,32,768]{2,1,0:T(8,128)(2,1)S(1)} all-to-all(bf16[8,32,768]{2,1,0:T(8,128)(2,1)S(1)} %gelu_rows.1), channel_id=1, replica_groups=mesh['row'=8,'col'=8,'x'=4,'core'=2] {'row'}, dimensions={0} | all-to-all | bytes 786432 | tf_op jit(solution)/shard_map/all_to_all | solution.py:39
  73.1 2.1 %output_terms.1 = bf16[256,1536]{1,0:T(8,128)(2,1)} custom-call(bf16[256,768]{1,0:T(8,128)(2,1)S(1)} %bitcast.5, bf16[1536,384]{1,0:T(8,128)(2,1)S(1)} %copy-done, bf16[384,1536]{1,0:T(8,128)(2,1)S(1)} %copy-done.1, bf16[1536,384]{1,0:T(8,128)(2,1)S(1)} %collective-permute-done.refs_3_, bf16[384,1536]{1,0:T(8,128)(2,1)S(1)} %collective-permute-done.1.refs_4_), custom_call_target="tpu_custom_call" | custom-call | flops 603979776 | bytes 5898240 | tf_op jit(solution)/shard_map/output_terms/pallas_call | solution.py:45
  75.2 9.4 %all-to-all-start.4 = ((bf16[32,8,1536]{2,1,0:T(8,128)(2,1)}), bf16[32,8,1536]{2,1,0:T(8,128)(2,1)S(1)}, u32[]{:S(2)}, u32[]{:S(2)}) async-start(bf16[32,8,1536]{2,1,0:T(8,128)(2,1)} %bitcast.12), calls=%async_computation.4 | async-start | bytes 1572864 | tf_op jit(solution)/shard_map/all_to_all | solution.py:39
  84.7 1.9 %collective-permute-start.2 = (bf16[256,384]{1,0:T(8,128)(2,1)S(1)}, bf16[256,384]{1,0:T(8,128)(2,1)S(1)}, u32[]{:S(2)}, u32[]{:S(2)}) collective-permute-start(bf16[256,384]{1,0:T(8,128)(2,1)S(1)} %get-tuple-element.23), channel_id=1, source_target_pairs={{0,1},{1,0},{2,3},{3,2},{4,5},{5,4},{6,7},{7,6},{8,9},{9,8},{10,11... | collective-permute-start | bytes 589832 | tf_op jit(solution)/shard_map/ppermute | solution.py:35
  86.6 1.4 %collective-permute-done.2.refs_3_ = bf16[256,384]{1,0:T(8,128)(2,1)S(1)} collective-permute-done((bf16[256,384]{1,0:T(8,128)(2,1)S(1)}, bf16[256,384]{1,0:T(8,128)(2,1)S(1)}, u32[]{:S(2)}, u32[]{:S(2)}) %collective-permute-start.2) | collective-permute-done | bytes 196640 | tf_op jit(solution)/shard_map/ppermute | solution.py:35
  88.0 2.0 %collective-permute-start.3 = (bf16[256,1536]{1,0:T(8,128)(2,1)S(1)}, bf16[256,1536]{1,0:T(8,128)(2,1)S(1)}, u32[]{:S(2)}, u32[]{:S(2)}) collective-permute-start(bf16[256,1536]{1,0:T(8,128)(2,1)S(1)} %bitcast.8), channel_id=1, source_target_pairs={{0,1},{1,0},{2,3},{3,2},{4,5},{5,4},{6,7},{7,6},{8,9},{9,8},{10,11... | collective-permute-start | bytes 2359304 | tf_op jit(solution)/shard_map/ppermute | solution.py:35
  90.1 2.1 %collective-permute-done.3.refs_1_ = bf16[256,1536]{1,0:T(8,128)(2,1)S(1)} collective-permute-done((bf16[256,1536]{1,0:T(8,128)(2,1)S(1)}, bf16[256,1536]{1,0:T(8,128)(2,1)S(1)}, u32[]{:S(2)}, u32[]{:S(2)}) %collective-permute-start.3) | collective-permute-done | bytes 786464 | tf_op jit(solution)/shard_map/ppermute | solution.py:35
  92.2 2.2 %weight_gradients.1 = (bf16[1536,384]{1,0:T(8,128)(2,1)}, bf16[384,1536]{1,0:T(8,128)(2,1)}) custom-call(bf16[256,1536]{1,0:T(8,128)(2,1)S(1)} %bitcast.9, bf16[256,1536]{1,0:T(8,128)(2,1)S(1)} %collective-permute-done.3.refs_1_, bf16[256,384]{1,0:T(8,128)(2,1)S(1)} %get-tuple-element.22.refs_2_, bf16[256,384]{1,0:T(8,128)(2,1)S(1)} %collective-permute-done.2.refs_3_), custom_call_target="tpu_custom_call" | custom-call | flops 603979776 | bytes 4325376 | tf_op jit(solution)/shard_map/weight_gradients/pallas_call | solution.py:45
  94.4 10.3 %all-to-all-done.4 = bf16[32,8,1536]{2,1,0:T(8,128)(2,1)S(1)} async-done(((bf16[32,8,1536]{2,1,0:T(8,128)(2,1)}), bf16[32,8,1536]{2,1,0:T(8,128)(2,1)S(1)}, u32[]{:S(2)}, u32[]{:S(2)}) %all-to-all-start.4) | async-done | bytes 786464 | tf_op jit(solution)/shard_map/all_to_all | solution.py:39
  104.7 0.1 reduce_sum.12
  104.8 0.6 fusion.1
  (1 shorter events, 0.0 us)
Async XLA Ops:
  0.6 13.3 %collective-permute-start = (bf16[1536,384]{1,0:T(8,128)(2,1)}, bf16[1536,384]{1,0:T(8,128)(2,1)S(1)}, u32[]{:S(2)}, u32[]{:S(2)}) collective-permute-start(bf16[1536,384]{1,0:T(8,128)(2,1)} %refs_1_.3), channel_id=1, source_target_pairs={{0,1},{1,0},{2,3},{3,2},{4,5},{5,4},{6,7},{7,6},{8,9},{9,8},{10,11... | collective-permute-start | bytes 3538952 | tf_op jit(solution)/shard_map/ppermute | solution.py:35
  4.0 19.6 %all-to-all-start = ((bf16[8,8,1536]{2,1,0:T(8,128)(2,1)}), bf16[8,8,1536]{2,1,0:T(8,128)(2,1)S(1)}, u32[]{:S(2)}, u32[]{:S(2)}) async-start(bf16[8,8,1536]{2,1,0:T(8,128)(2,1)} %broadcast_in_dim.2), calls=%async_computation | async-start | bytes 393216 | tf_op jit(solution)/shard_map/all_to_all | solution.py:39
  14.0 24.7 %collective-permute-start.1 = (bf16[384,1536]{1,0:T(8,128)(2,1)}, bf16[384,1536]{1,0:T(8,128)(2,1)S(1)}, u32[]{:S(2)}, u32[]{:S(2)}) collective-permute-start(bf16[384,1536]{1,0:T(8,128)(2,1)} %refs_2_.3), channel_id=1, source_target_pairs={{0,1},{1,0},{2,3},{3,2},{4,5},{5,4},{6,7},{7,6},{8,9},{9,8},{10,11... | collective-permute-start | bytes 3538952 | tf_op jit(solution)/shard_map/ppermute | solution.py:35
  23.6 15.0 %copy-start.1 = (bf16[384,1536]{1,0:T(8,128)(2,1)S(1)}, bf16[384,1536]{1,0:T(8,128)(2,1)}, u32[]{:S(2)}) copy-start(bf16[384,1536]{1,0:T(8,128)(2,1)} %refs_2_.3) | copy-start | bytes 3538948
  23.7 14.9 %copy-start = (bf16[1536,384]{1,0:T(8,128)(2,1)S(1)}, bf16[1536,384]{1,0:T(8,128)(2,1)}, u32[]{:S(2)}) copy-start(bf16[1536,384]{1,0:T(8,128)(2,1)} %refs_1_.3) | copy-start | bytes 3538948
  75.2 29.5 %all-to-all-start.4 = ((bf16[32,8,1536]{2,1,0:T(8,128)(2,1)}), bf16[32,8,1536]{2,1,0:T(8,128)(2,1)S(1)}, u32[]{:S(2)}, u32[]{:S(2)}) async-start(bf16[32,8,1536]{2,1,0:T(8,128)(2,1)} %bitcast.12), calls=%async_computation.4 | async-start | bytes 1572864 | tf_op jit(solution)/shard_map/all_to_all | solution.py:39
  84.7 3.3 %collective-permute-start.2 = (bf16[256,384]{1,0:T(8,128)(2,1)S(1)}, bf16[256,384]{1,0:T(8,128)(2,1)S(1)}, u32[]{:S(2)}, u32[]{:S(2)}) collective-permute-start(bf16[256,384]{1,0:T(8,128)(2,1)S(1)} %get-tuple-element.23), channel_id=1, source_target_pairs={{0,1},{1,0},{2,3},{3,2},{4,5},{5,4},{6,7},{7,6},{8,9},{9,8},{10,11... | collective-permute-start | bytes 589832 | tf_op jit(solution)/shard_map/ppermute | solution.py:35
  88.0 4.2 %collective-permute-start.3 = (bf16[256,1536]{1,0:T(8,128)(2,1)S(1)}, bf16[256,1536]{1,0:T(8,128)(2,1)S(1)}, u32[]{:S(2)}, u32[]{:S(2)}) collective-permute-start(bf16[256,1536]{1,0:T(8,128)(2,1)S(1)} %bitcast.8), channel_id=1, source_target_pairs={{0,1},{1,0},{2,3},{3,2},{4,5},{5,4},{6,7},{7,6},{8,9},{9,8},{10,11... | collective-permute-start | bytes 2359304 | tf_op jit(solution)/shard_map/ppermute | solution.py:35
